TPU v7x, 512 devices: a whole 4x8x8 slice. The times are simulated.
512 devices in a mesh: ctx: 32 (over x, y), kvh: 8 (over z_lo, core), grp: 2 (over z_hi).
Axes of the slice: x: 4, y: 8, z: 8 (z_hi: 2, z_lo: 4; z = z_hi * 4 + z_lo), core: 2. Of those that a mesh axis runs over, the one named last changes fastest.
Arguments:
- hidden_in: bfloat16 [2, 32, 8192], P(None, None, ('ctx', 'grp')), may hold values from -16 to 16
- norm_gain: bfloat16 [8192], P(('ctx', 'grp')), may hold values from 0.5 to 1.5
- w_qkv: bfloat16 [8192, 8, 1280], P(('ctx', 'grp'), 'kvh'), may hold values from -0.0625 to 0.0625
- qkv_bias: bfloat16 [8, 1280], P('kvh'), may hold values from -40 to 40
- kv_pool: bfloat16 [2, 2, 8, 16384, 128], P('grp', None, 'kvh', 'ctx'), may hold values from -16 to 16
- suffix_lengths: int32 [32], P('ctx'), may hold values from 1 to 512, 8192 in all
- w_out: bfloat16 [8192, 8192], P('kvh', ('ctx', 'grp')), may hold values from -0.0625 to 0.0625
Outputs:
- attention_out: bfloat16 [2, 32, 8192], P(None, None, ('ctx', 'grp'))
Inputs may be any that keep to these rules, and one draw needn't show every extreme that they name: `suffix_lengths`: they sum to 8192, and one of them is 512.
All inputs are finite; a program needn't handle non-finite values. No bound on the sum of `suffix_lengths` on one device may be relied on, other than what follows from the above.
Results may differ from a plain program's by a relative error of at most 0.018.
Values may be sent and summed in bfloat16 or wider, within the bound.
A program may use at most 128 MiB of HBM per device.

v0:
```python
import math

import jax
import jax.numpy as jnp
from jax import lax
from jax.sharding import PartitionSpec as P

NORM_EPS = 1e-06
FLOOR_SCORE = -1e30


def merged_2(value, axis, join):
    pieces = jax.tree.map(lambda part: lax.all_gather(part, axis), value)
    head = jax.tree.map(lambda part: part[0], pieces)
    tail = jax.tree.map(lambda part: part[1:], pieces)
    running, _ = lax.scan(lambda running, slab: (join(running, slab), None), head, tail)
    return running


def merge_parts(first, second):
    best_score = jnp.maximum(first[0], second[0])
    fade_first = jnp.exp(first[0] - best_score)
    fade_second = jnp.exp(second[0] - best_score)
    return (
        best_score,
        first[1] * fade_first + second[1] * fade_second,
        first[2] * fade_first[..., None] + second[2] * fade_second[..., None],
    )


def prefix_part(queries, keys, values):
    slot_count = keys.shape[1]
    factor = 1.0 / math.sqrt(keys.shape[2])
    stride = math.gcd(slot_count, 512)
    part_shape = queries.shape[:3]

    def advance(position, carry):
        best_score, weight_sum, summed = carry
        scores = (
            jnp.einsum("qkgd,ksd->qkgs", queries, keys, preferred_element_type=jnp.float32) * factor
        )
        raised = jnp.maximum(best_score, jnp.max(scores, axis=-1))
        fade_out = jnp.exp(best_score - raised)
        weights = jnp.exp(scores - raised[..., None]).astype(jnp.bfloat16)
        weight_sum = weight_sum * fade_out + jnp.sum(weights.astype(jnp.float32), axis=-1)
        summed = summed * fade_out[..., None] + jnp.einsum(
            "qkgs,ksd->qkgd", weights, values, preferred_element_type=jnp.float32
        )
        return (raised, weight_sum, summed)

    start = (
        jnp.full(part_shape, FLOOR_SCORE, jnp.float32),
        jnp.zeros(part_shape, jnp.float32),
        jnp.zeros(queries.shape, jnp.float32),
    )
    return lax.fori_loop(0, slot_count // stride, advance, start)


def local(hidden_in, norm_gain, w_qkv, qkv_bias, kv_pool, suffix_lengths, w_out):
    step_count, batch_rows, local_width = hidden_in.shape
    heads_local = w_qkv.shape[1]
    group_width = w_qkv.shape[2]
    head_width = kv_pool.shape[-1]
    query_groups = group_width // head_width - 2
    own_rows = suffix_lengths.shape[0]
    span_devices = lax.axis_size("ctx") * lax.axis_size("grp")
    full_width = local_width * span_devices
    page_index = lax.axis_index("grp")
    slot_count = kv_pool.shape[3]
    suffix_slots = slot_count // own_rows
    widened = hidden_in.astype(jnp.float32)
    squares = lax.psum(jnp.sum(widened * widened, axis=-1), ("ctx", "grp"))
    inverse = lax.rsqrt(squares / full_width + NORM_EPS)
    normed = (widened * inverse[..., None] * norm_gain.astype(jnp.float32)).astype(jnp.bfloat16)
    normed = normed.reshape(step_count * batch_rows, local_width)
    weights_flat = w_qkv.reshape(local_width, heads_local * group_width)
    projected = lax.psum_scatter(
        jnp.dot(normed, weights_flat, preferred_element_type=jnp.float32),
        ("ctx", "grp"),
        scatter_dimension=0,
        tiled=True,
    )
    own_share = (projected + qkv_bias.reshape(-1).astype(jnp.float32)).astype(jnp.bfloat16)
    gathered = lax.all_gather(own_share, ("ctx", "grp"), axis=0, tiled=True)
    gathered = gathered.reshape(step_count * batch_rows, heads_local, query_groups + 2, head_width)
    queries = gathered[:, :, :query_groups]
    new_keys = gathered[:, :, query_groups]
    new_values = gathered[:, :, query_groups + 1]
    row_start = lax.axis_index("ctx") * own_rows

    def suffix_part():
        factor = 1.0 / math.sqrt(head_width)
        query_rows = lax.dynamic_slice_in_dim(
            queries.reshape(step_count, batch_rows, heads_local, query_groups, head_width),
            row_start,
            own_rows,
            1,
        )
        key_rows = lax.dynamic_slice_in_dim(
            new_keys.reshape(step_count, batch_rows, heads_local, head_width),
            row_start,
            own_rows,
            1,
        )
        value_rows = lax.dynamic_slice_in_dim(
            new_values.reshape(step_count, batch_rows, heads_local, head_width),
            row_start,
            own_rows,
            1,
        )
        cached_keys = kv_pool[0, 0].reshape(heads_local, own_rows, suffix_slots, head_width)
        cached_values = kv_pool[0, 1].reshape(heads_local, own_rows, suffix_slots, head_width)
        cache_scores = (
            jnp.einsum(
                "trkgd,krsd->trkgs", query_rows, cached_keys, preferred_element_type=jnp.float32
            )
            * factor
        )
        fresh_scores = (
            jnp.einsum(
                "trkgd,urkd->trkgu", query_rows, key_rows, preferred_element_type=jnp.float32
            )
            * factor
        )
        live_slots = (jnp.arange(suffix_slots)[None, :] < suffix_lengths[:, None])[
            None, :, None, None, :
        ]
        causal = (jnp.arange(step_count)[None, :] <= jnp.arange(step_count)[:, None])[
            :, None, None, None, :
        ]
        cache_scores = jnp.where(live_slots, cache_scores, FLOOR_SCORE)
        fresh_scores = jnp.where(causal, fresh_scores, FLOOR_SCORE)
        best_score = jnp.maximum(jnp.max(cache_scores, axis=-1), jnp.max(fresh_scores, axis=-1))
        cache_weights = jnp.exp(cache_scores - best_score[..., None]).astype(jnp.bfloat16)
        fresh_weights = jnp.exp(fresh_scores - best_score[..., None]).astype(jnp.bfloat16)
        weight_sum = jnp.sum(cache_weights.astype(jnp.float32), axis=-1) + jnp.sum(
            fresh_weights.astype(jnp.float32), axis=-1
        )
        summed = jnp.einsum(
            "trkgs,krsd->trkgd", cache_weights, cached_values, preferred_element_type=jnp.float32
        )
        summed = summed + jnp.einsum(
            "trkgu,urkd->trkgd", fresh_weights, value_rows, preferred_element_type=jnp.float32
        )

        def place_rows(member, filler):
            padded = jnp.full((step_count, batch_rows) + member.shape[2:], filler, jnp.float32)
            padded = lax.dynamic_update_slice_in_dim(padded, member, row_start, 1)
            return padded.reshape((step_count * batch_rows,) + member.shape[2:])

        return (
            place_rows(best_score, FLOOR_SCORE),
            place_rows(weight_sum, 0.0),
            place_rows(summed, 0.0),
        )

    def prefix_whole():
        return prefix_part(queries, kv_pool[0, 0], kv_pool[0, 1])

    best_part, total_part, summed_part = lax.cond(page_index == 0, prefix_whole, suffix_part)
    merged = merged_2((best_part, total_part, summed_part), ("ctx", "grp"), merge_parts)
    attended = (
        (merged[2] / merged[1][..., None]).astype(jnp.bfloat16).reshape(step_count * batch_rows, -1)
    )
    projected_out = jnp.dot(attended, w_out, preferred_element_type=jnp.float32)
    summed_out = lax.psum(projected_out.astype(jnp.bfloat16), "kvh")
    return summed_out.reshape(step_count, batch_rows, local_width)


def solution(mesh):
    placed = (
        P(None, None, ("ctx", "grp")),
        P(("ctx", "grp")),
        P(("ctx", "grp"), "kvh", None),
        P("kvh", None),
        P("grp", None, "kvh", "ctx", None),
        P("ctx"),
        P("kvh", ("ctx", "grp")),
    )
    return jax.shard_map(
        local, mesh=mesh, in_specs=placed, out_specs=P(None, None, ("ctx", "grp")), check_vma=False
    )
```

profile of v0, /device:TPU:1, one launch (start us, length us, event | category | flops | bytes accessed | tf_op | source)
XLA Modules:
  0.0 1906.8 jit_solution(14439641617985464655)
XLA Ops:
  8.1 202.2 %psum.14 = f32[2,32]{1,0:T(2,128)S(1)} all-reduce(f32[2,32]{1,0:T(2,128)S(1)} %fusion.44), channel_id=1, replica_groups=mesh['ctx'=32,'kvh'=8,'grp'=2] {'ctx','grp'}, use_global_device_ids=true, to_apply=%region_1.0 | all-reduce | flops 64 | bytes 512 | tf_op jit(solution)/shard_map/psum | solution.py:72
  212.1 1.3 dynamic-slice
  213.4 787.9 %all-reduce.3.cloned.1.call-done = f32[64,1280]{1,0:T(8,128)} async-done(((f32[64,1280]{1,0:T(8,128)}), f32[64,1280]{1,0:T(8,128)}) %all-reduce.3.cloned.1.call-update) | async-done | bytes 327696
  1001.2 1.4 fusion.48
  1002.7 189.3 %all-gather.3 = bf16[64,1,1280]{2,1,0:T(2,128)(2,1)S(1)} all-gather(bf16[1,1,1280]{2,1,0:T(2,128)(2,1)S(1)} %fusion.48), channel_id=1, replica_groups=mesh['ctx'=32,'kvh'=8,'grp'=2] {'ctx','grp'}, dimensions={0}, use_global_device_ids=true | all-gather | bytes 166400 | tf_op jit(solution)/shard_map/all_gather | solution.py:84
  1193.1 1.4 conditional.1
  1195.2 215.4 %all-gather = f32[4096,1,8]{2,1,0:T(1,128)S(1)} all-gather(f32[64,1,8]{2,1,0:T(1,128)S(1)} %get-tuple-element.91), channel_id=2, replica_groups=mesh['ctx'=32,'kvh'=8,'grp'=2] {'ctx','grp'}, dimensions={0}, use_global_device_ids=true | all-gather | bytes 133120 | tf_op jit(solution)/shard_map/all_gather | solution.py:13
  1410.6 1.3 copy-done.1
  1412.0 245.5 %all-gather.1 = f32[4096,1,8]{2,1,0:T(1,128)S(1)} all-gather(f32[64,1,8]{2,1,0:T(1,128)S(1)} %get-tuple-element.92), channel_id=3, replica_groups=mesh['ctx'=32,'kvh'=8,'grp'=2] {'ctx','grp'}, dimensions={0}, use_global_device_ids=true | all-gather | bytes 133120 | tf_op jit(solution)/shard_map/all_gather | solution.py:13
  1657.5 1.9 slice.61
  1660.4 2.2 copy.86
  1662.6 11.3 slice.62
  1673.8 91.2 %while.14 = (s32[]{:T(128)}, f32[64,1,8]{0,2,1:T(8,128)S(1)}, f32[64,1,8]{0,2,1:T(8,128)S(1)}, f32[64,1,8,128]{3,2,1,0:T(8,128)S(1)}, f32[63,64,1,8]{1,3,2,0:T(8...) while((s32[]{:T(128)}, f32[64,1,8]{0,2,1:T(8,128)S(1)}, ...), condition=%wide.region_12.13_spmd, body=%wide.region_11.0_spmd.sunk | while | flops 200194 | bytes 825449 | solution.py:16
  1674.1 1.2 fusion.59
  1675.5 1.2 fusion.59
  1677.0 1.2 fusion.59
  1678.4 1.2 fusion.59
  1684.2 1.2 fusion.59
  1701.6 1.2 fusion.59
  1711.7 1.2 fusion.59
  1729.1 1.2 fusion.59
  1739.2 1.2 fusion.59
  1756.6 1.2 fusion.59
  1765.4 134.5 %psum.15 = bf16[2,32,128]{2,1,0:T(8,128)(2,1)} all-reduce(bf16[2,32,128]{2,1,0:T(8,128)(2,1)S(1)} %bitcast.178), channel_id=1, replica_groups=mesh['ctx'=32,'kvh'=8,'grp'=2] {'kvh'}, use_global_device_ids=true, to_apply=%region_13.14 | all-reduce | flops 8192 | bytes 32768 | tf_op jit(solution)/shard_map/psum | solution.py:166
  (411 shorter events, 84.5 us)
Async XLA Ops:
  6.5 204.5 %copy-start = (bf16[128,1,1280]{2,0,1:T(8,128)(2,1)S(1)}, bf16[128,1,1280]{2,0,1:T(8,128)(2,1)}, u32[]{:S(2)}) copy-start(bf16[128,1,1280]{2,0,1:T(8,128)(2,1)} %param.13) | copy-start | bytes 983044
  6.5 1186.5 %copy-start.3 = (bf16[1,2,1,512,128]{4,3,2,1,0:T(8,128)(2,1)S(1)}, bf16[1,2,1,512,128]{4,3,2,1,0:T(8,128)(2,1)}, u32[]{:S(2)}) copy-start(bf16[1,2,1,512,128]{4,3,2,1,0:T(8,128)(2,1)} %param.15) | copy-start | bytes 786436
  6.5 994.7 %all-reduce.3.cloned.1.call-start = ((), (), s32[]{:S(2)}) async-start(), calls=%async_computation.1 | async-start | bytes 655360
  212.0 1450.5 %all-gather.6.cloned.1.call-start = ((), (), s32[]{:S(2)}) async-start(), calls=%async_computation | async-start | bytes 17039360 | tf_op jit(solution)/shard_map/all_gather | solution.py:13
  1194.5 0.7 copy-start.2
  1410.6 1.4 copy-start.1
  1657.5 1.9 slice-start.1
  1657.5 2.2 slice-start.2
  1662.6 11.3 slice-start
  1673.8 91.4 %copy-start.4 = (bf16[1024,128]{1,0:T(8,128)(2,1)S(1)}, bf16[1024,128]{1,0:T(8,128)(2,1)}, u32[]{:S(2)}) copy-start(bf16[1024,128]{1,0:T(8,128)(2,1)} %param.17) | copy-start | bytes 786436
Sparse Core Ops, SparseCore 0:
  212.2 789.0 all-reduce.2
  1195.4 428.1 all-gather.5
where the time goes:
time: 1910 us
  blocking collectives  987 us (52%)
  waiting for transfers between devices  788 us (41%)
  other arithmetic  83.1 us (4%)
  local copies, waits for them, and re-layouts  30.9 us (2%)
    unnamed x3, waiting for transfers between devices  788 us
    all_gather x2, blocking collectives, merged_2(): pieces = jax.tree.map(lambda part: lax.all_gather(part, axis), value)  461 us
    psum x1, blocking collectives, local(): squares = lax.psum(jnp.sum(widened * widened, axis=-1), ('ctx', 'grp'))  202 us
    all_gather x1, blocking collectives, local(): gathered = lax.all_gather(own_share, ('ctx', 'grp'), axis=0, tiled=True)  189 us
    psum x1, blocking collectives, local(): summed_out = lax.psum(projected_out.astype(jnp.bfloat16), 'kvh')  134 us
    add x63, other arithmetic, merge_parts(): first[2] * fade_first[..., None] + second[2] * fade_second[..., None]  76 us
  transfers between devices with their start and end apart: 2, of which 1 were waited for; matrix products, arithmetic and copies ran while one was open for 0% of the time, Pallas kernels for 0%

commit v1 on v0

v1 whole, which is shorter than its diff:
```python
import functools
import math

import jax
import jax.numpy as jnp
from jax import lax
from jax.experimental import pallas as pl
from jax.experimental.pallas import tpu as pltpu
from jax.sharding import PartitionSpec as P

NORM_EPS = 1e-06
FLOOR_SCORE = -1e30
MESH = pl.DeviceIdType.MESH
NX, NY = 4, 8
HD = 128
F32, BF16 = jnp.float32, jnp.bfloat16


def zigzag(k, middle):
    return middle + (1 - 2 * lax.rem(k, 2)) * ((k + 1) // 2)


def wait_bytes(buffer, sem):
    pltpu.make_async_copy(buffer, buffer, sem).wait()


def total(parts):
    return functools.reduce(jnp.add, parts)


def kernel(
    h_any, gain_any, w_any, bias_any, kv_any, len_ref, wo_any, out_ref,
    h_v, gain_v, w_v, bias_v, kv_v, wo_v,
    part, part_in, sq, sq_in,
    mid, mid_in, newkv_in, sq2, sq2_in,
    query, o_out, o_in, lse_out, lse_in, att, res,
    local_sem, send_sem, recv_sem,
):
    ctx, kvh, grp = lax.axis_index("ctx"), lax.axis_index("kvh"), lax.axis_index("grp")
    x, y = ctx // NY, lax.rem(ctx, NY)
    factor = 1.0 / math.sqrt(HD)

    def send(src, dst, phase, target):
        pltpu.make_async_remote_copy(
            src_ref=src, dst_ref=dst, send_sem=send_sem.at[phase], recv_sem=recv_sem.at[phase],
            device_id=target, device_id_type=MESH,
        ).start()

    loads = [
        pltpu.make_async_copy(src, dst, local_sem.at[i])
        for i, (src, dst) in enumerate(
            ((h_any, h_v), (gain_any, gain_v), (w_any, w_v), (bias_any, bias_v), (kv_any, kv_v.at[3]), (wo_any, wo_v))
        )
    ]
    for load in loads:
        load.start()

    def x_peer(i):
        return lax.rem(x + 1 + i, NX)

    def plane_peer(i):
        return lax.rem(y + zigzag(i // 2, 4), NY), lax.rem(grp + 1 - lax.rem(i, 2), 2)

    def y_peer(i):
        return lax.rem(y + zigzag(i, 4), NY)

    def ctx_peer(i):
        return lax.rem(x + zigzag(lax.rem(i, 4), 2), NX) * NY + lax.rem(y + zigzag(i // 4, 4), NY)

    def kvh_peer(i):
        return lax.rem(kvh + 1 + i, 8)

    barrier = pltpu.get_barrier_semaphore()

    def hello(device):
        pl.semaphore_signal(barrier, inc=1, device_id=device, device_id_type=MESH)

    @pl.loop(0, 31)
    def _(i):
        hello({"ctx": ctx_peer(i)})

    @pl.loop(0, 8)
    def _(i):
        hello({"ctx": x * NY + lax.rem(y + i, NY), "grp": 1 - grp})

    @pl.loop(0, 7)
    def _(i):
        hello({"kvh": kvh_peer(i)})

    loads[0].wait()
    loads[1].wait()
    h = h_v[...].astype(F32)
    h = jnp.concatenate([h[t, 8 * b : 8 * b + 8] for b in range(NX) for t in range(2)], axis=0)
    gain = gain_v[...].astype(F32).reshape(1, HD)
    scaled = (h * gain).astype(BF16)
    squares = jnp.sum(h * h, axis=1, keepdims=True)
    lane = lax.broadcasted_iota(jnp.int32, (64, HD), 1)
    row = lax.broadcasted_iota(jnp.int32, (64, HD), 0)
    sq[...] = jnp.sum(jnp.where(lane == row, squares, 0.0), axis=0, keepdims=True)
    loads[2].wait()
    for c in range(5):
        prod = jnp.dot(scaled, w_v[:, 256 * c : 256 * c + 256], preferred_element_type=F32).astype(BF16)
        for half in range(2):
            part[:, 2 * c + half] = prod[:, HD * half : HD * half + HD].reshape(NX, 16, HD)

    pl.semaphore_wait(barrier, 46)

    @pl.loop(0, 3)
    def _(i):
        to = x_peer(i)
        send(part.at[to], part_in.at[i], 0, {"ctx": to * NY + y})
        send(sq, sq_in.at[i], 1, {"ctx": to * NY + y})

    @pl.when(grp == 0)
    def _():
        @pl.loop(0, 3)
        def _(i):
            send(kv_any, kv_v.at[i], 2, {"ctx": x_peer(i) * NY + y})

    wait_bytes(part_in, recv_sem.at[0])
    wait_bytes(sq_in, recv_sem.at[1])
    mid[...] = (total([part_in[i].astype(F32) for i in range(3)]) + part[x].astype(F32)).astype(BF16)
    sq2[...] = total([sq_in[i] for i in range(3)]) + sq[...]

    @pl.loop(0, 15)
    def _(i):
        to_y, to_grp = plane_peer(i)
        to = {"ctx": x * NY + to_y, "grp": to_grp}
        send(mid.at[to_y], mid_in.at[i], 3, to)
        send(sq2, sq2_in.at[i], 5, to)

        @pl.when(to_grp == 1)
        def _():
            send(mid.at[pl.ds(8, 2)], newkv_in.at[i], 4, to)

    loads[3].wait()
    wait_bytes(sq2_in, recv_sem.at[5])
    lane = lax.broadcasted_iota(jnp.int32, (16, HD), 1)
    row = lax.broadcasted_iota(jnp.int32, (16, HD), 0)
    squares = total([sq2_in[i] for i in range(15)]) + sq2[...]
    squares = jnp.sum(jnp.where(lane == row + 16 * x, squares, 0.0), axis=1, keepdims=True)
    inverse = lax.rsqrt(squares / 8192.0 + NORM_EPS)
    wait_bytes(mid_in, recv_sem.at[3])
    summed = total([mid_in[i].astype(F32) for i in range(15)]) + mid[y].astype(F32)
    bias = bias_v[:, pl.ds(pl.multiple_of(y * HD, HD), HD)].astype(F32)
    query[y] = (summed * inverse + bias).astype(BF16)

    @pl.loop(0, 7)
    def _(i):
        send(query.at[y], query.at[y], 6, {"ctx": x * NY + y_peer(i)})

    loads[4].wait()
    wait_bytes(query.at[pl.ds(0, 7)], recv_sem.at[6])

    def finish(best, weight_sum, out, valid):
        lse = best + jnp.log(weight_sum)
        if valid is not None:
            lse = jnp.where(valid, lse, FLOOR_SCORE)
        o_out[...] = (out / weight_sum).astype(BF16).reshape(8, 16, HD)
        lane = lax.broadcasted_iota(jnp.int32, (HD, HD), 1)
        row = lax.broadcasted_iota(jnp.int32, (HD, HD), 0)
        lse_out[...] = jnp.sum(jnp.where(lane == row, lse, 0.0), axis=0, keepdims=True)

    def scores_of(q, keys):
        return lax.dot_general(q, keys, (((1,), (1,)), ((), ())), preferred_element_type=F32) * factor

    @pl.when(grp == 0)
    def _():
        wait_bytes(kv_v.at[pl.ds(0, 3)], recv_sem.at[2])
        q = query[...].reshape(HD, HD)
        scores = [scores_of(q, kv_v[i, 0]) for i in range(NX)]
        best = functools.reduce(jnp.maximum, [jnp.max(s, axis=1, keepdims=True) for s in scores])
        weights = [jnp.exp(s - best).astype(BF16) for s in scores]
        weight_sum = total([jnp.sum(w.astype(F32), axis=1, keepdims=True) for w in weights])
        out = total([jnp.dot(w, kv_v[i, 1], preferred_element_type=F32) for i, w in enumerate(weights)])
        finish(best, weight_sum, out, None)

    @pl.when(grp == 1)
    def _():
        wait_bytes(newkv_in, recv_sem.at[4])
        fresh = total([newkv_in[i].astype(F32) for i in range(15)]) + mid[8:10].astype(F32)
        new_bias = bias_v[:, 8 * HD :].astype(F32)
        new_keys = (fresh[0] * inverse + new_bias[:, :HD]).astype(BF16)
        new_values = (fresh[1] * inverse + new_bias[:, HD:]).astype(BF16)
        q = query[...].reshape(HD, HD)
        cached = scores_of(q, kv_v[3, 0])
        slot = lax.broadcasted_iota(jnp.int32, cached.shape, 1)
        cached = jnp.where(slot < len_ref[0], cached, FLOOR_SCORE)
        new = scores_of(q, new_keys)
        key_row = lax.broadcasted_iota(jnp.int32, new.shape, 1)
        q_row = lax.broadcasted_iota(jnp.int32, new.shape, 0)
        seen = (lax.rem(key_row, 8) == y) & (key_row // 8 <= lax.rem(q_row // 8, 2))
        new = jnp.where(seen, new, FLOOR_SCORE)
        best = jnp.maximum(jnp.max(cached, axis=1, keepdims=True), jnp.max(new, axis=1, keepdims=True))
        cached = jnp.exp(cached - best).astype(BF16)
        new = jnp.exp(new - best).astype(BF16)
        weight_sum = jnp.sum(cached.astype(F32), axis=1, keepdims=True) + jnp.sum(new.astype(F32), axis=1, keepdims=True)
        out = jnp.dot(cached, kv_v[3, 1], preferred_element_type=F32)
        out = out + jnp.dot(new, new_values, preferred_element_type=F32)
        own = lax.rem(lax.broadcasted_iota(jnp.int32, (HD, 1), 0), 8) == y
        finish(best, weight_sum, out, own)

    @pl.loop(0, 15)
    def _(i):
        to_y, to_grp = plane_peer(i)
        to = {"ctx": x * NY + to_y, "grp": to_grp}
        send(o_out.at[to_y], o_in.at[i], 7, to)
        send(lse_out, lse_in.at[i], 8, to)

    wait_bytes(lse_in, recv_sem.at[8])
    mine = lane == row + 16 * y
    lses = [lse_in[i] for i in range(15)] + [lse_out[...]]
    lses = [jnp.sum(jnp.where(mine, v, 0.0), axis=1, keepdims=True) for v in lses]
    best = functools.reduce(jnp.maximum, lses)
    shares = [jnp.exp(v - best) for v in lses]
    wait_bytes(o_in, recv_sem.at[7])
    outs = [o_in[i].astype(F32) for i in range(15)] + [o_out[y].astype(F32)]
    joined = total([o * s for o, s in zip(outs, shares)]) / total(shares)
    own = y * NX + x
    att[own] = joined.astype(BF16)

    @pl.loop(0, 31)
    def _(i):
        send(att.at[own], att.at[own], 9, {"ctx": ctx_peer(i)})

    loads[5].wait()
    wait_bytes(att.at[pl.ds(0, 31)], recv_sem.at[9])
    projected = total(
        [
            jnp.dot(att[4 * j : 4 * j + 4].reshape(64, HD), wo_v[HD * j : HD * j + HD], preferred_element_type=F32)
            for j in range(8)
        ]
    )
    ordered = [projected[16 * b + 8 * t : 16 * b + 8 * t + 8] for t in range(2) for b in range(NX)]
    res[kvh] = jnp.concatenate(ordered, axis=0).astype(BF16)

    @pl.loop(0, 7)
    def _(i):
        send(res.at[kvh], res.at[kvh], 10, {"kvh": kvh_peer(i)})

    wait_bytes(part_in, send_sem.at[0])
    wait_bytes(sq_in, send_sem.at[1])
    wait_bytes(mid_in, send_sem.at[3])
    wait_bytes(sq2_in, send_sem.at[5])

    @pl.when(grp == 0)
    def _():
        wait_bytes(kv_v.at[pl.ds(0, 3)], send_sem.at[2])
        wait_bytes(newkv_in.at[pl.ds(0, 8)], send_sem.at[4])

    @pl.when(grp == 1)
    def _():
        wait_bytes(newkv_in.at[pl.ds(0, 7)], send_sem.at[4])

    wait_bytes(query.at[pl.ds(0, 7)], send_sem.at[6])
    wait_bytes(o_in, send_sem.at[7])
    wait_bytes(lse_in, send_sem.at[8])
    wait_bytes(att.at[pl.ds(0, 31)], send_sem.at[9])
    wait_bytes(res.at[pl.ds(0, 7)], send_sem.at[10])
    wait_bytes(res.at[pl.ds(0, 7)], recv_sem.at[10])
    out_ref[...] = total([res[k].astype(F32) for k in range(8)]).astype(BF16).reshape(2, 32, HD)


def local(hidden_in, norm_gain, w_qkv, qkv_bias, kv_pool, suffix_lengths, w_out):
    anywhere = pl.BlockSpec(memory_space=pl.ANY)
    vmem = pltpu.VMEM
    return pl.pallas_call(
        kernel,
        out_shape=jax.ShapeDtypeStruct((2, 32, HD), BF16),
        in_specs=[anywhere] * 5 + [pl.BlockSpec(memory_space=pltpu.SMEM), anywhere],
        out_specs=pl.BlockSpec(memory_space=vmem),
        scratch_shapes=[
            vmem((2, 32, HD), BF16), vmem((HD,), BF16), vmem((HD, 1280), BF16), vmem((1, 1280), BF16),
            vmem((4, 2, 512, HD), BF16), vmem((1024, HD), BF16),
            vmem((4, 10, 16, HD), BF16), vmem((3, 10, 16, HD), BF16), vmem((1, HD), F32), vmem((3, 1, HD), F32),
            vmem((10, 16, HD), BF16), vmem((15, 16, HD), BF16), vmem((15, 2, 16, HD), BF16),
            vmem((1, HD), F32), vmem((15, 1, HD), F32),
            vmem((8, 16, HD), BF16), vmem((8, 16, HD), BF16), vmem((15, 16, HD), BF16),
            vmem((1, HD), F32), vmem((15, 1, HD), F32), vmem((32, 16, HD), BF16), vmem((8, 64, HD), BF16),
            pltpu.SemaphoreType.DMA((6,)), pltpu.SemaphoreType.DMA((11,)), pltpu.SemaphoreType.DMA((11,)),
        ],
        compiler_params=pltpu.CompilerParams(
            collective_id=0, has_side_effects=True, vmem_limit_bytes=60 << 20
        ),
        name="attention_block",
    )(
        hidden_in, norm_gain, w_qkv.reshape(HD, 1280), qkv_bias, kv_pool.reshape(2, 512, HD),
        suffix_lengths, w_out,
    )


def solution(mesh):
    placed = (
        P(None, None, ("ctx", "grp")),
        P(("ctx", "grp")),
        P(("ctx", "grp"), "kvh", None),
        P("kvh", None),
        P("grp", None, "kvh", "ctx", None),
        P("ctx"),
        P("kvh", ("ctx", "grp")),
    )
    return jax.shard_map(
        local, mesh=mesh, in_specs=placed, out_specs=P(None, None, ("ctx", "grp")), check_vma=False
    )
```

time: 1910 us -> 60.7 us (0.03)
  blocking collectives: 987 us -> 0 us
  waiting for transfers between devices: 788 us -> 0 us
  other arithmetic: 83.1 us -> 0 us
  Pallas kernels: 0 us -> 58.6 us
  local copies, waits for them, and re-layouts: 30.9 us -> 1.32 us
    unnamed x3 -> x0, waiting for transfers between devices: 788 us -> none
    all_gather x3 -> x0, blocking collectives: 650 us -> none  [the longest x2 461 us: merged_2(): pieces = jax.tree.map(lambda part: lax.all_gather(part, axis), value)]
    psum x2 -> x0, blocking collectives: 337 us -> none  [the longest x1 202 us: local(): squares = lax.psum(jnp.sum(widened * widened, axis=-1), ('ctx', 'grp'))]
    add x64 -> x0, other arithmetic: 76 us -> none  [the longest x63 76 us: merge_parts(): first[2] * fade_first[..., None] + second[2] * fade_second[..., None]]
    pallas_call x0 -> x1, Pallas kernels: none -> 58.6 us  [local(): pl.pallas_call(kernel, out_shape=jax.ShapeDtypeStruct((2, 32, HD), BF16),...]
  transfers between devices with their start and end apart: 2 -> 0, of which waited for: 1 -> 0; matrix products, arithmetic and copies ran while one was open for 0% -> 0% of each run, Pallas kernels for 0% -> 0%
where the time goes in v1:
time: 60.7 us; the launch traced here: 60.5 us
  Pallas kernels  58.6 us (97%)
  local copies, waits for them, and re-layouts  1.32 us (2%)
  between operations  0.66 us (1%)
    pallas_call x1, Pallas kernels, local(): pl.pallas_call(kernel, out_shape=jax.ShapeDtypeStruct((2, 32, HD), BF16),...  58.6 us
    unnamed x1, local copies, waits for them, and re-layouts  1.32 us

profile of v1, /device:TPU:1, one launch (start us, length us, event | category | flops | bytes accessed | tf_op | source)
XLA Modules:
  0.0 60.5 jit_solution(729637274404884921)
XLA Ops:
  0.7 58.6 %attention_block.1 = bf16[2,32,128]{2,1,0:T(8,128)(2,1)} custom-call(bf16[2,32,128]{2,1,0:T(8,128)(2,1)} %h_any.1, bf16[128]{0:T(256)(128)(2,1)} %gain_any.1, bf16[128,1280]{1,0:T(8,128)(2,1)} %bitcast.2, bf16[1,1280]{1,0:T(2,128)(2,1)} %bias_any.1, bf16[2,512,128]{2,1,0:T(8,128)(2,1)} %bitcast.3, s32[1]{0:T(128)S(6)} %copy.9.len_ref, bf16[1024,128]{1,0:T(8,128)(2,1)} %wo_any.1), custom_call_target="tpu_custom_call" | custom-call | tf_op jit(solution)/shard_map/attention_block/pallas_call | solution.py:267
  59.2 1.3 %copy.10 = bf16[2,32,128]{2,1,0:T(8,128)(2,1)} copy(bf16[2,32,128]{2,1,0:T(8,128)(2,1)} %attention_block.1) | data formatting | bytes 32768

commit v2 on v1

v2 whole, which is shorter than its diff:
```python
import functools
import math

import jax
import jax.numpy as jnp
from jax import lax
from jax.experimental import pallas as pl
from jax.experimental.pallas import tpu as pltpu
from jax.sharding import PartitionSpec as P

NORM_EPS = 1e-06
FLOOR_SCORE = -1e30
MESH = pl.DeviceIdType.MESH
NX, NY = 4, 8
HD = 128
F32, BF16 = jnp.float32, jnp.bfloat16


def zigzag(k, middle):
    return middle + (1 - 2 * lax.rem(k, 2)) * ((k + 1) // 2)


def wait_bytes(buffer, sem):
    pltpu.make_async_copy(buffer, buffer, sem).wait()


def total(parts):
    return functools.reduce(jnp.add, parts)


def kernel(
    h_any, gain_any, w_any, bias_any, kv_any, len_ref, wo_any, out_ref,
    h_v, gain_v, w_v, bias_v, kv_v, wo_v, head_bias,
    part, part_in, sq, sq_in, direct_in, direct_sq_in,
    mid, mid_in, rows, pairs, pairs_in, sq2, sq2_in,
    query, o_out, o_in, lse_out, lse_in, suf_out, suf_in, att, res,
    local_sem, send_sem, recv_sem, hello_sem,
):
    ctx, kvh, grp = lax.axis_index("ctx"), lax.axis_index("kvh"), lax.axis_index("grp")
    x, y = ctx // NY, lax.rem(ctx, NY)
    factor = 1.0 / math.sqrt(HD)

    def send(src, dst, phase, target):
        pltpu.make_async_remote_copy(
            src_ref=src, dst_ref=dst, send_sem=send_sem.at[phase], recv_sem=recv_sem.at[phase],
            device_id=target, device_id_type=MESH,
        ).start()

    loads = [
        pltpu.make_async_copy(src, dst, local_sem.at[i])
        for i, (src, dst) in enumerate(
            ((h_any, h_v), (gain_any, gain_v), (w_any, w_v), (bias_any, bias_v), (kv_any, kv_v.at[3]), (wo_any, wo_v))
        )
    ]
    for load in loads:
        load.start()

    def x_peer(i):
        return lax.rem(x + zigzag(i, 2), NX) * NY + y

    def y_peer(i):
        return lax.rem(y + zigzag(i, 4), NY)

    def column(to_y):
        return x * NY + to_y

    def plane_peer(i):
        return lax.rem(x + zigzag(lax.rem(i, 4), 2), NX), lax.rem(y + zigzag(i // 4, 4), NY)

    def kvh_peer(i):
        return lax.rem(kvh + 1 + i, 8)

    barrier = pltpu.get_barrier_semaphore()

    def greet(device):
        pl.semaphore_signal(barrier, inc=1, device_id=device, device_id_type=MESH)

    @pl.loop(0, 3)
    def _(i):
        greet({"ctx": x_peer(i)})

    @pl.loop(0, 7)
    def _(i):
        greet({"kvh": kvh_peer(i)})

    @pl.loop(0, 7)
    def _(i):
        greet({"ctx": column(y_peer(i))})

    @pl.when(grp == 0)
    def _():
        @pl.loop(0, 32)
        def _(i):
            greet({"ctx": i, "grp": 1})

    loads[0].wait()
    loads[1].wait()
    h = h_v[...].astype(F32)
    h = jnp.concatenate([h[t, 8 * b : 8 * b + 8] for b in range(NX) for t in range(2)], axis=0)
    gain = gain_v[...].astype(F32).reshape(1, HD)
    scaled = (h * gain).astype(BF16)
    squares = jnp.sum(h * h, axis=1, keepdims=True)
    lane = lax.broadcasted_iota(jnp.int32, (64, HD), 1)
    row = lax.broadcasted_iota(jnp.int32, (64, HD), 0)
    sq[...] = jnp.sum(jnp.where(lane == row, squares, 0.0), axis=0, keepdims=True)
    loads[2].wait()
    for c in range(5):
        prod = jnp.dot(scaled, w_v[:, 256 * c : 256 * c + 256], preferred_element_type=F32).astype(BF16)
        for half in range(2):
            part[:, 2 * c + half] = prod[:, HD * half : HD * half + HD].reshape(NX, 16, HD)

    @pl.when(grp == 0)
    def _():
        pl.semaphore_wait(barrier, 17)

    @pl.when(grp == 1)
    def _():
        pl.semaphore_wait(barrier, 49)

        @pl.loop(0, 8)
        def _(i):
            there = {"ctx": column(y_peer(i)), "grp": 0}
            pl.semaphore_signal(hello_sem, inc=1, device_id=there, device_id_type=MESH)

        @pl.loop(0, 32)
        def _(i):
            to_x, to_y = plane_peer(i)
            to = {"ctx": to_x * NY + to_y, "grp": 0}
            send(part.at[to_x, to_y], direct_in.at[ctx], 6, to)
            send(sq, direct_sq_in.at[ctx], 7, to)

    @pl.loop(0, 3)
    def _(i):
        to = x_peer(i)
        send(part.at[to // NY], part_in.at[i], 0, {"ctx": to})
        send(sq, sq_in.at[i], 1, {"ctx": to})

    @pl.when(grp == 0)
    def _():
        @pl.loop(0, 3)
        def _(i):
            send(kv_any, kv_v.at[i], 2, {"ctx": x_peer(i)})

    rows[...] = jnp.zeros_like(rows)
    loads[3].wait()
    for j in range(8):
        head_bias[j : j + 1] = bias_v[:, HD * j : HD * j + HD].astype(F32)
    head_bias[8:16] = head_bias[0:8]
    head_bias[16:24] = jnp.broadcast_to(bias_v[:, 8 * HD : 9 * HD].astype(F32), (8, HD))
    head_bias[24:32] = jnp.broadcast_to(bias_v[:, 9 * HD :].astype(F32), (8, HD))
    wait_bytes(sq_in, recv_sem.at[1])
    sq2[...] = total([sq_in[i] for i in range(3)]) + sq[...]
    wait_bytes(part_in, recv_sem.at[0])
    line = total([part_in[i].astype(F32) for i in range(3)]) + part[x].astype(F32)

    @pl.when(grp == 0)
    def _():
        mid[...] = line.astype(BF16)

        @pl.loop(0, 7)
        def _(i):
            to_y = y_peer(i)
            send(mid.at[to_y], mid_in.at[i], 3, {"ctx": column(to_y)})
            send(sq2, sq2_in.at[i], 5, {"ctx": column(to_y)})

    rows[0:144] = line[0:9].reshape(144, HD)
    rows[192:208] = line[9]
    for b in range(8):
        pieces = [rows[pl.ds(b + first, 8, stride=step)] for first, step in ((0, 16), (8, 16), (128, 8), (192, 8))]
        pairs[b] = jnp.concatenate(pieces, axis=0).astype(BF16)

    @pl.when(grp == 0)
    def _():
        pl.semaphore_wait(hello_sem, 8)

        @pl.loop(0, 8)
        def _(i):
            to_y = y_peer(i)
            to = {"ctx": column(to_y), "grp": 1}
            send(pairs.at[to_y], pairs_in.at[7 + i], 4, to)
            send(sq2, sq2_in.at[7 + i], 5, to)

        lane = lax.broadcasted_iota(jnp.int32, (16, HD), 1)
        row = lax.broadcasted_iota(jnp.int32, (16, HD), 0)
        wait_bytes(sq2_in.at[pl.ds(0, 7)], recv_sem.at[5])
        wait_bytes(mid_in, recv_sem.at[3])
        squares = total([sq2_in[i] for i in range(7)]) + sq2[...]
        summed = total([mid_in[i].astype(F32) for i in range(7)]) + mid[y].astype(F32)
        bias = bias_v[:, pl.ds(pl.multiple_of(y * HD, HD), HD)].astype(F32)
        wait_bytes(direct_sq_in, recv_sem.at[7])
        squares = total([direct_sq_in[i] for i in range(32)]) + squares
        squares = jnp.sum(jnp.where(lane == row + 16 * x, squares, 0.0), axis=1, keepdims=True)
        inverse = lax.rsqrt(squares / 8192.0 + NORM_EPS)
        wait_bytes(direct_in, recv_sem.at[6])
        summed = total([direct_in[i].astype(F32) for i in range(32)]) + summed
        query[y] = (summed * inverse + bias).astype(BF16)

        @pl.loop(0, 7)
        def _(i):
            send(query.at[y], query.at[y], 8, {"ctx": column(y_peer(i))})

    @pl.when(grp == 1)
    def _():
        @pl.loop(0, 7)
        def _(i):
            to_y = y_peer(i)
            send(pairs.at[to_y], pairs_in.at[i], 4, {"ctx": column(to_y)})
            send(sq2, sq2_in.at[i], 5, {"ctx": column(to_y)})

    def scores_of(q, keys):
        return lax.dot_general(q, keys, (((1,), (1,)), ((), ())), preferred_element_type=F32) * factor

    @pl.when(grp == 0)
    def _():
        loads[4].wait()
        wait_bytes(kv_v.at[pl.ds(0, 3)], recv_sem.at[2])
        wait_bytes(query.at[pl.ds(0, 7)], recv_sem.at[8])
        q = query[...].reshape(HD, HD)
        scores = [scores_of(q, kv_v[i, 0]) for i in range(NX)]
        best = functools.reduce(jnp.maximum, [jnp.max(s, axis=1, keepdims=True) for s in scores])
        weights = [jnp.exp(s - best).astype(BF16) for s in scores]
        weight_sum = total([jnp.sum(w.astype(F32), axis=1, keepdims=True) for w in weights])
        out = total([jnp.dot(w, kv_v[i, 1], preferred_element_type=F32) for i, w in enumerate(weights)])
        o_out[...] = (out / weight_sum).astype(BF16).reshape(8, 16, HD)
        lse = best + jnp.log(weight_sum)
        lane = lax.broadcasted_iota(jnp.int32, (HD, HD), 1)
        row = lax.broadcasted_iota(jnp.int32, (HD, HD), 0)
        lse_out[...] = jnp.sum(jnp.where(lane == row, lse, 0.0), axis=0, keepdims=True)

        @pl.loop(0, 15)
        def _(i):
            to_y, to_grp = y_peer(i // 2), 1 - lax.rem(i, 2)
            to = {"ctx": column(to_y), "grp": to_grp}
            send(o_out.at[to_y], o_in.at[y], 9, to)
            send(lse_out, lse_in.at[y], 10, to)

        o_in[y] = o_out[y]
        lse_in[y] = lse_out[...]

    @pl.when(grp == 1)
    def _():
        lane = lax.broadcasted_iota(jnp.int32, (32, HD), 1)
        row = lax.broadcasted_iota(jnp.int32, (32, HD), 0)
        step = jnp.where(row < 16, row // 8, lax.rem(row, 2))
        wait_bytes(sq2_in, recv_sem.at[5])
        squares = total([sq2_in[i] for i in range(15)]) + sq2[...]
        squares = jnp.sum(jnp.where(lane == 16 * x + 8 * step + y, squares, 0.0), axis=1, keepdims=True)
        inverse = lax.rsqrt(squares / 8192.0 + NORM_EPS)
        wait_bytes(pairs_in, recv_sem.at[4])
        summed = total([pairs_in[i].astype(F32) for i in range(15)]) + pairs[y].astype(F32)
        summed = (summed * inverse + head_bias[...]).astype(BF16)
        loads[4].wait()
        q = summed[0:16]
        fresh = summed[16:32]
        cached = scores_of(q, kv_v[3, 0])
        slot = lax.broadcasted_iota(jnp.int32, cached.shape, 1)
        cached = jnp.where(slot < len_ref[0], cached, FLOOR_SCORE)
        new = scores_of(q, fresh)
        key_step = lax.broadcasted_iota(jnp.int32, new.shape, 1)
        q_step = lax.broadcasted_iota(jnp.int32, new.shape, 0) // 8
        new = jnp.where(key_step <= q_step, new, FLOOR_SCORE)
        best = jnp.maximum(jnp.max(cached, axis=1, keepdims=True), jnp.max(new, axis=1, keepdims=True))
        cached = jnp.exp(cached - best).astype(BF16)
        new = jnp.exp(new - best).astype(BF16)
        weight_sum = jnp.sum(cached.astype(F32), axis=1, keepdims=True) + jnp.sum(new.astype(F32), axis=1, keepdims=True)
        out = jnp.dot(cached, kv_v[3, 1], preferred_element_type=F32)
        values = jnp.concatenate([summed[24:32].astype(F32), jnp.zeros((8, HD), F32)], axis=0).astype(BF16)
        out = out + jnp.dot(new, values, preferred_element_type=F32)
        out = out / weight_sum
        lse = jnp.broadcast_to(best + jnp.log(weight_sum), (16, HD))
        for t in range(2):
            suf_out[pl.ds(t, 8, stride=8)] = out[8 * t : 8 * t + 8]
            suf_out[pl.ds(2 + t, 8, stride=8)] = lse[8 * t : 8 * t + 8]
        zero = jnp.zeros((8, HD), F32)
        for t in range(4, 8):
            suf_out[pl.ds(t, 8, stride=8)] = zero

        @pl.loop(0, 15)
        def _(i):
            to_y, to_grp = y_peer(i // 2), lax.rem(i, 2)
            to = {"ctx": column(to_y), "grp": to_grp}
            send(suf_out.at[pl.ds(pl.multiple_of(8 * to_y, 8), 8)], suf_in.at[pl.ds(pl.multiple_of(8 * y, 8), 8)], 11, to)

        mine = pl.ds(pl.multiple_of(8 * y, 8), 8)
        suf_in[mine] = suf_out[mine]

    @pl.when(grp == 0)
    def _():
        wait_bytes(lse_in.at[pl.ds(0, 7)], recv_sem.at[10])
        wait_bytes(suf_in, recv_sem.at[11])
        wait_bytes(o_in.at[pl.ds(0, 7)], recv_sem.at[9])

    @pl.when(grp == 1)
    def _():
        wait_bytes(lse_in, recv_sem.at[10])
        wait_bytes(suf_in.at[pl.ds(0, 56)], recv_sem.at[11])
        wait_bytes(o_in, recv_sem.at[9])

    lane = lax.broadcasted_iota(jnp.int32, (16, HD), 1)
    row = lax.broadcasted_iota(jnp.int32, (16, HD), 0)
    mine = lane == row + 16 * y
    lses = [jnp.sum(jnp.where(mine, lse_in[i], 0.0), axis=1, keepdims=True) for i in range(8)]
    lses.append(jnp.concatenate([suf_in[pl.ds(2 + t, 8, stride=8)] for t in range(2)], axis=0)[:, 0:1])
    best = functools.reduce(jnp.maximum, lses)
    shares = [jnp.exp(v - best) for v in lses]
    outs = [o_in[i].astype(F32) for i in range(8)]
    outs.append(jnp.concatenate([suf_in[pl.ds(t, 8, stride=8)] for t in range(2)], axis=0))
    joined = total([o * s for o, s in zip(outs, shares)]) / total(shares)
    own = y * NX + x
    att[own] = joined.astype(BF16)

    @pl.loop(0, 31)
    def _(i):
        to_x, to_y = plane_peer(i)
        send(att.at[own], att.at[own], 12, {"ctx": to_x * NY + to_y})

    loads[5].wait()
    wait_bytes(att.at[pl.ds(0, 31)], recv_sem.at[12])
    projected = total(
        [
            jnp.dot(att[4 * j : 4 * j + 4].reshape(64, HD), wo_v[HD * j : HD * j + HD], preferred_element_type=F32)
            for j in range(8)
        ]
    )
    ordered = [projected[16 * b + 8 * t : 16 * b + 8 * t + 8] for t in range(2) for b in range(NX)]
    res[kvh] = jnp.concatenate(ordered, axis=0).astype(BF16)

    @pl.loop(0, 7)
    def _(i):
        send(res.at[kvh], res.at[kvh], 13, {"kvh": kvh_peer(i)})


    @pl.when(grp == 1)
    def _():
        wait_bytes(direct_in, send_sem.at[6])
        wait_bytes(direct_sq_in, send_sem.at[7])

    wait_bytes(part_in, send_sem.at[0])
    wait_bytes(sq_in, send_sem.at[1])

    @pl.when(grp == 0)
    def _():
        wait_bytes(kv_v.at[pl.ds(0, 3)], send_sem.at[2])

    @pl.when(grp == 0)
    def _():
        wait_bytes(mid_in, send_sem.at[3])
        wait_bytes(sq2_in, send_sem.at[5])
        wait_bytes(pairs_in.at[pl.ds(0, 8)], send_sem.at[4])
        wait_bytes(query.at[pl.ds(0, 7)], send_sem.at[8])

    @pl.when(grp == 1)
    def _():
        wait_bytes(sq2_in.at[pl.ds(0, 7)], send_sem.at[5])
        wait_bytes(pairs_in.at[pl.ds(0, 7)], send_sem.at[4])

    @pl.when(grp == 0)
    def _():
        wait_bytes(o_in, send_sem.at[9])
        wait_bytes(o_in.at[pl.ds(0, 7)], send_sem.at[9])
        wait_bytes(lse_in, send_sem.at[10])
        wait_bytes(lse_in.at[pl.ds(0, 7)], send_sem.at[10])

    @pl.when(grp == 1)
    def _():
        wait_bytes(suf_in, send_sem.at[11])
        wait_bytes(suf_in.at[pl.ds(0, 56)], send_sem.at[11])

    wait_bytes(att.at[pl.ds(0, 31)], send_sem.at[12])
    wait_bytes(res.at[pl.ds(0, 7)], send_sem.at[13])
    wait_bytes(res.at[pl.ds(0, 7)], recv_sem.at[13])
    out_ref[...] = total([res[k].astype(F32) for k in range(8)]).astype(BF16).reshape(2, 32, HD)


def local(hidden_in, norm_gain, w_qkv, qkv_bias, kv_pool, suffix_lengths, w_out):
    anywhere = pl.BlockSpec(memory_space=pl.ANY)
    vmem = pltpu.VMEM
    return pl.pallas_call(
        kernel,
        out_shape=jax.ShapeDtypeStruct((2, 32, HD), BF16),
        in_specs=[anywhere] * 5 + [pl.BlockSpec(memory_space=pltpu.SMEM), anywhere],
        out_specs=pl.BlockSpec(memory_space=vmem),
        scratch_shapes=[
            vmem((2, 32, HD), BF16), vmem((HD,), BF16), vmem((HD, 1280), BF16), vmem((1, 1280), BF16),
            vmem((4, 2, 512, HD), BF16), vmem((1024, HD), BF16), vmem((32, HD), F32),
            vmem((4, 10, 16, HD), BF16), vmem((3, 10, 16, HD), BF16), vmem((1, HD), F32), vmem((3, 1, HD), F32),
            vmem((32, 16, HD), BF16), vmem((32, 1, HD), F32),
            vmem((10, 16, HD), BF16), vmem((7, 16, HD), BF16), vmem((256, HD), F32),
            vmem((8, 32, HD), BF16), vmem((15, 32, HD), BF16), vmem((1, HD), F32), vmem((15, 1, HD), F32),
            vmem((8, 16, HD), BF16), vmem((8, 16, HD), BF16), vmem((8, 16, HD), BF16),
            vmem((1, HD), F32), vmem((8, 1, HD), F32), vmem((64, HD), F32), vmem((64, HD), F32),
            vmem((32, 16, HD), BF16), vmem((8, 64, HD), BF16),
            pltpu.SemaphoreType.DMA((6,)), pltpu.SemaphoreType.DMA((14,)), pltpu.SemaphoreType.DMA((14,)),
            pltpu.SemaphoreType.REGULAR,
        ],
        compiler_params=pltpu.CompilerParams(
            collective_id=0, has_side_effects=True, vmem_limit_bytes=60 << 20
        ),
        name="attention_block",
    )(
        hidden_in, norm_gain, w_qkv.reshape(HD, 1280), qkv_bias, kv_pool.reshape(2, 512, HD),
        suffix_lengths, w_out,
    )


def solution(mesh):
    placed = (
        P(None, None, ("ctx", "grp")),
        P(("ctx", "grp")),
        P(("ctx", "grp"), "kvh", None),
        P("kvh", None),
        P("grp", None, "kvh", "ctx", None),
        P("ctx"),
        P("kvh", ("ctx", "grp")),
    )
    return jax.shard_map(
        local, mesh=mesh, in_specs=placed, out_specs=P(None, None, ("ctx", "grp")), check_vma=False
    )
```

time: 60.7 us -> 50.6 us (0.83)
  Pallas kernels: 58.6 us -> 48.3 us
    pallas_call x1, Pallas kernels: 58.6 us -> 48.3 us  [local(): pl.pallas_call(kernel, out_shape=jax.ShapeDtypeStruct((2, 32, HD), BF16),...]
where the time goes in v2:
time: 50.6 us; the launch traced here: 50.3 us
  Pallas kernels  48.3 us (95%)
  local copies, waits for them, and re-layouts  1.32 us (3%)
  between operations  0.66 us (1%)
    pallas_call x1, Pallas kernels, local(): pl.pallas_call(kernel, out_shape=jax.ShapeDtypeStruct((2, 32, HD), BF16),...  48.3 us
    unnamed x1, local copies, waits for them, and re-layouts  1.32 us

profile of v2, /device:TPU:1, one launch (start us, length us, event | category | flops | bytes accessed | tf_op | source)
XLA Modules:
  0.0 50.3 jit_solution(18100125649910544524)
XLA Ops:
  0.7 48.3 %attention_block.1 = bf16[2,32,128]{2,1,0:T(8,128)(2,1)} custom-call(bf16[2,32,128]{2,1,0:T(8,128)(2,1)} %h_any.1, bf16[128]{0:T(256)(128)(2,1)} %gain_any.1, bf16[128,1280]{1,0:T(8,128)(2,1)} %bitcast.2, bf16[1,1280]{1,0:T(2,128)(2,1)} %bias_any.1, bf16[2,512,128]{2,1,0:T(8,128)(2,1)} %bitcast.3, s32[1]{0:T(128)S(6)} %copy.9.len_ref, bf16[1024,128]{1,0:T(8,128)(2,1)} %wo_any.1), custom_call_target="tpu_custom_call" | custom-call | tf_op jit(solution)/shard_map/attention_block/pallas_call | solution.py:378
  49.0 1.3 %copy.10 = bf16[2,32,128]{2,1,0:T(8,128)(2,1)} copy(bf16[2,32,128]{2,1,0:T(8,128)(2,1)} %attention_block.1) | data formatting | bytes 32768

commit v3 on v1

v3 whole, which is shorter than its diff:
```python
import functools
import math

import jax
import jax.numpy as jnp
from jax import lax
from jax.experimental import pallas as pl
from jax.experimental.pallas import tpu as pltpu
from jax.sharding import PartitionSpec as P

NORM_EPS = 1e-06
FLOOR_SCORE = -1e30
MESH = pl.DeviceIdType.MESH
NX, NY = 4, 8
HD = 128
F32, BF16 = jnp.float32, jnp.bfloat16


def zigzag(k, middle):
    return middle + (1 - 2 * lax.rem(k, 2)) * ((k + 1) // 2)


def wait_bytes(buffer, sem):
    pltpu.make_async_copy(buffer, buffer, sem).wait()


def total(parts):
    return functools.reduce(jnp.add, parts)


def kernel(
    h_any, gain_any, w_any, bias_any, kv_any, len_ref, wo_any, out_ref,
    h_v, gain_v, w_v, bias_v, kv_v, wo_v, head_bias, rows,
    part, part_in, sq, sq_in, direct_in, direct_sq_in,
    mid, mid_in, pairs, pairs_in, sq2, sq2_in,
    query, o_out, o_in, lse_out, lse_in, suf_out, suf_in, att, res,
    local_sem, send_sem, recv_sem, flag,
):
    ctx, kvh, grp = lax.axis_index("ctx"), lax.axis_index("kvh"), lax.axis_index("grp")
    x, y = ctx // NY, lax.rem(ctx, NY)
    z, core = kvh // 2, lax.rem(kvh, 2)
    lead = kvh - core + 1
    factor = 1.0 / math.sqrt(HD)
    first, late = grp == 0, grp == 1
    helper, worker = core == 0, core == 1

    def send(src, dst, phase, target):
        pltpu.make_async_remote_copy(
            src_ref=src, dst_ref=dst, send_sem=send_sem.at[phase], recv_sem=recv_sem.at[phase],
            device_id=target, device_id_type=MESH,
        ).start()

    loads = [
        pltpu.make_async_copy(src, dst, local_sem.at[i])
        for i, (src, dst) in enumerate(
            ((h_any, h_v), (gain_any, gain_v), (w_any, w_v), (bias_any, bias_v), (kv_any, kv_v.at[1, 3]), (wo_any, wo_v.at[1]))
        )
    ]
    for load in loads[:4]:
        load.start()

    def x_peer(i):
        return lax.rem(x + zigzag(i, 2), NX) * NY + y

    def y_peer(i):
        return lax.rem(y + zigzag(i, 4), NY)

    def column(to_y):
        return x * NY + to_y

    def plane_peer(i):
        return lax.rem(x + zigzag(lax.rem(i, 4), 2), NX), lax.rem(y + zigzag(i // 4, 4), NY)

    def z_peer(i):
        return lax.rem(z + 1 + i, 4) * 2

    barrier = pltpu.get_barrier_semaphore()

    def tell(sem, device):
        pl.semaphore_signal(sem, inc=1, device_id=device, device_id_type=MESH)

    hello, plane, go, ready, last = (flag.at[i] for i in range(5))

    @pl.when(worker)
    def _():
        @pl.loop(0, 3)
        def _(i):
            tell(barrier, {"ctx": x_peer(i)})

        @pl.loop(0, 4)
        def _(i):
            tell(barrier, {"ctx": x_peer(i), "kvh": lead - 1})

    @pl.when(worker & first)
    def _():
        @pl.loop(0, 7)
        def _(i):
            tell(barrier, {"ctx": column(y_peer(i))})

        @pl.loop(0, 3)
        def _(i):
            tell(barrier, {"kvh": z_peer(i) + 1})

    @pl.when(worker)
    def _():
        loads[4].start()
        loads[5].start()

    @pl.when(worker & first)
    def _():
        pl.semaphore_wait(barrier, 13)

        @pl.loop(0, 7)
        def _(i):
            tell(plane, {"ctx": column(y_peer(i))})

        pl.semaphore_wait(plane, 7)
        tell(barrier, {"grp": 1})
        tell(barrier, {"grp": 1, "kvh": lead - 1})

    @pl.when(helper & first)
    def _():
        pl.semaphore_wait(barrier, 4)

    loads[0].wait()
    loads[1].wait()
    h = h_v[...].astype(F32)
    h = jnp.concatenate([h[t, 8 * b : 8 * b + 8] for b in range(NX) for t in range(2)], axis=0)
    gain = gain_v[...].astype(F32).reshape(1, HD)
    scaled = (h * gain).astype(BF16)
    squares = jnp.sum(h * h, axis=1, keepdims=True)
    lane = lax.broadcasted_iota(jnp.int32, (64, HD), 1)
    row = lax.broadcasted_iota(jnp.int32, (64, HD), 0)
    sq[...] = jnp.sum(jnp.where(lane == row, squares, 0.0), axis=0, keepdims=True)
    loads[2].wait()
    for c in range(5):
        prod = jnp.dot(scaled, w_v[:, 256 * c : 256 * c + 256], preferred_element_type=F32).astype(BF16)
        for half in range(2):
            part[:, 2 * c + half] = prod[:, HD * half : HD * half + HD].reshape(NX, 16, HD)

    @pl.when(worker & late)
    def _():
        pl.semaphore_wait(barrier, 4)

        @pl.loop(0, 8)
        def _(i):
            tell(hello, {"ctx": column(y_peer(i)), "grp": 0})

    @pl.when(helper & late)
    def _():
        pl.semaphore_wait(barrier, 5)
        tell(hello, {"kvh": lead, "grp": 0})

    @pl.loop(0, 3)
    def _(i):
        to = x_peer(i)
        send(part.at[to // NY], part_in.at[core, i], 0, {"ctx": to, "kvh": lead})

    @pl.when(helper)
    def _():
        send(part.at[x], part_in.at[core, 3], 1, {"kvh": lead})

    @pl.when(worker)
    def _():
        @pl.loop(0, 3)
        def _(i):
            send(sq, sq_in.at[i], 8, {"ctx": x_peer(i)})

    @pl.when(late)
    def _():
        @pl.loop(0, 32)
        def _(i):
            to_x, to_y = plane_peer(i)
            send(part.at[to_x, to_y], direct_in.at[core, ctx], 6, {"ctx": to_x * NY + to_y, "kvh": lead, "grp": 0})

    @pl.when(late & worker)
    def _():
        @pl.loop(0, 32)
        def _(i):
            to_x, to_y = plane_peer(i)
            send(sq, direct_sq_in.at[ctx], 7, {"ctx": to_x * NY + to_y, "grp": 0})

    loads[3].wait()
    for j in range(8):
        head_bias[1, j : j + 1] = bias_v[:, HD * j : HD * j + HD].astype(F32)
    head_bias[1, 8:16] = head_bias[1, 0:8]
    head_bias[1, 16:24] = jnp.broadcast_to(bias_v[:, 8 * HD : 9 * HD].astype(F32), (8, HD))
    head_bias[1, 24:32] = jnp.broadcast_to(bias_v[:, 9 * HD :].astype(F32), (8, HD))

    @pl.when(helper)
    def _():
        own = {"kvh": lead}
        send(head_bias.at[1], head_bias.at[0], 2, own)

        @pl.when(late)
        def _():
            send(kv_any, kv_v.at[0, 3], 3, own)

    @pl.when(first)
    def _():
        @pl.loop(0, 3)
        def _(i):
            send(kv_any, kv_v.at[core, i], 4, {"ctx": x_peer(i), "kvh": lead})

    @pl.when(helper)
    def _():
        own = {"kvh": lead}

        @pl.when(first)
        def _():
            send(kv_any, kv_v.at[0, 3], 3, own)

        send(wo_any, wo_v.at[0], 5, own)

    @pl.when(worker)
    def _():
        rows[...] = jnp.zeros_like(rows)
        wait_bytes(sq_in, recv_sem.at[8])
        sq2[...] = total([sq_in[i] for i in range(3)]) + sq[...]
        wait_bytes(part_in.at[0, 3], recv_sem.at[1])
        wait_bytes(part_in.at[:, pl.ds(0, 3)], recv_sem.at[0])
        lines = [
            total([part_in[0, i].astype(F32) for i in range(4)]),
            total([part_in[1, i].astype(F32) for i in range(3)]) + part[x].astype(F32),
        ]

        @pl.when(first)
        def _():
            for head, line in enumerate(lines):
                mid[:, head] = line[0:8].astype(BF16)

            @pl.loop(0, 7)
            def _(i):
                to_y = y_peer(i)
                send(mid.at[to_y], mid_in.at[i], 9, {"ctx": column(to_y)})
                send(sq2, sq2_in.at[i], 10, {"ctx": column(to_y)})

        for head, line in enumerate(lines):
            rows[head, 0:144] = line[0:9].reshape(144, HD)
            rows[head, 192:208] = line[9]
            for b in range(8):
                pieces = [rows[head, pl.ds(b + at, 8, stride=step)] for at, step in ((0, 16), (8, 16), (128, 8), (192, 8))]
                pairs[b, head] = jnp.concatenate(pieces, axis=0).astype(BF16)

        @pl.when(first)
        def _():
            pl.semaphore_wait(hello, 9)
            tell(go, {"grp": 1})

            @pl.loop(0, 8)
            def _(i):
                to_y = y_peer(i)
                to = {"ctx": column(to_y), "grp": 1}
                send(pairs.at[to_y], pairs_in.at[7 + i], 11, to)
                send(sq2, sq2_in.at[7 + i], 10, to)

            @pl.loop(0, 3)
            def _(i):
                tell(ready, {"kvh": z_peer(i) + 1})

            lane = lax.broadcasted_iota(jnp.int32, (16, HD), 1)
            row = lax.broadcasted_iota(jnp.int32, (16, HD), 0)
            wait_bytes(sq2_in.at[pl.ds(0, 7)], recv_sem.at[10])
            wait_bytes(mid_in, recv_sem.at[9])
            wait_bytes(head_bias.at[0], recv_sem.at[2])
            squares = total([sq2_in[i] for i in range(7)]) + sq2[...]
            sums = [total([mid_in[i, head].astype(F32) for i in range(7)]) + mid[y, head].astype(F32) for head in range(2)]
            pl.semaphore_wait(ready, 3)
            tell(last, {"grp": 1})
            wait_bytes(direct_sq_in, recv_sem.at[7])
            squares = total([direct_sq_in[i] for i in range(32)]) + squares
            squares = jnp.sum(jnp.where(lane == row + 16 * x, squares, 0.0), axis=1, keepdims=True)
            inverse = lax.rsqrt(squares / 8192.0 + NORM_EPS)
            wait_bytes(direct_in, recv_sem.at[6])
            for head in range(2):
                summed = total([direct_in[head, i].astype(F32) for i in range(32)]) + sums[head]
                query[y, head] = (summed * inverse + head_bias[head, pl.ds(y, 1)]).astype(BF16)

            @pl.loop(0, 7)
            def _(i):
                send(query.at[y], query.at[y], 12, {"ctx": column(y_peer(i))})

        @pl.when(late)
        def _():
            pl.semaphore_wait(go, 1)

            @pl.loop(0, 7)
            def _(i):
                to_y = y_peer(i)
                send(pairs.at[to_y], pairs_in.at[i], 11, {"ctx": column(to_y)})
                send(sq2, sq2_in.at[i], 10, {"ctx": column(to_y)})

        loads[4].wait()

        def scores_of(q, keys):
            return lax.dot_general(q, keys, (((1,), (1,)), ((), ())), preferred_element_type=F32) * factor

        @pl.when(first)
        def _():
            lane = lax.broadcasted_iota(jnp.int32, (HD, HD), 1)
            row = lax.broadcasted_iota(jnp.int32, (HD, HD), 0)
            wait_bytes(kv_v.at[:, pl.ds(0, 3)], recv_sem.at[4])
            wait_bytes(kv_v.at[0, 3], recv_sem.at[3])
            wait_bytes(query.at[pl.ds(0, 7)], recv_sem.at[12])
            for head in range(2):
                q = query[:, head].reshape(HD, HD)
                scores = [scores_of(q, kv_v[head, i, 0]) for i in range(NX)]
                best = functools.reduce(jnp.maximum, [jnp.max(s, axis=1, keepdims=True) for s in scores])
                weights = [jnp.exp(s - best).astype(BF16) for s in scores]
                weight_sum = total([jnp.sum(w.astype(F32), axis=1, keepdims=True) for w in weights])
                out = total([jnp.dot(w, kv_v[head, i, 1], preferred_element_type=F32) for i, w in enumerate(weights)])
                o_out[:, head] = (out / weight_sum).astype(BF16).reshape(8, 16, HD)
                lse = best + jnp.log(weight_sum)
                lse_out[head] = jnp.sum(jnp.where(lane == row, lse, 0.0), axis=0, keepdims=True)

            @pl.loop(0, 15)
            def _(i):
                to_y, to_grp = y_peer(i // 2), 1 - lax.rem(i, 2)
                to = {"ctx": column(to_y), "grp": to_grp}
                send(o_out.at[to_y], o_in.at[y], 13, to)
                send(lse_out, lse_in.at[y], 14, to)

            o_in[y] = o_out[y]
            lse_in[y] = lse_out[...]

        @pl.when(late)
        def _():
            lane = lax.broadcasted_iota(jnp.int32, (32, HD), 1)
            row = lax.broadcasted_iota(jnp.int32, (32, HD), 0)
            step = jnp.where(row < 16, row // 8, lax.rem(row, 2))
            wait_bytes(head_bias.at[0], recv_sem.at[2])
            wait_bytes(kv_v.at[0, 3], recv_sem.at[3])
            wait_bytes(sq2_in, recv_sem.at[10])
            squares = total([sq2_in[i] for i in range(15)]) + sq2[...]
            squares = jnp.sum(jnp.where(lane == 16 * x + 8 * step + y, squares, 0.0), axis=1, keepdims=True)
            inverse = lax.rsqrt(squares / 8192.0 + NORM_EPS)
            wait_bytes(pairs_in, recv_sem.at[11])
            for head in range(2):
                summed = total([pairs_in[i, head].astype(F32) for i in range(15)]) + pairs[y, head].astype(F32)
                summed = (summed * inverse + head_bias[head]).astype(BF16)
                q = summed[0:16]
                fresh = summed[16:32]
                cached = scores_of(q, kv_v[head, 3, 0])
                slot = lax.broadcasted_iota(jnp.int32, cached.shape, 1)
                cached = jnp.where(slot < len_ref[0], cached, FLOOR_SCORE)
                new = scores_of(q, fresh)
                key_step = lax.broadcasted_iota(jnp.int32, new.shape, 1)
                q_step = lax.broadcasted_iota(jnp.int32, new.shape, 0) // 8
                new = jnp.where(key_step <= q_step, new, FLOOR_SCORE)
                best = jnp.maximum(jnp.max(cached, axis=1, keepdims=True), jnp.max(new, axis=1, keepdims=True))
                cached = jnp.exp(cached - best).astype(BF16)
                new = jnp.exp(new - best).astype(BF16)
                weight_sum = jnp.sum(cached.astype(F32), axis=1, keepdims=True) + jnp.sum(
                    new.astype(F32), axis=1, keepdims=True
                )
                out = jnp.dot(cached, kv_v[head, 3, 1], preferred_element_type=F32)
                values = jnp.concatenate([summed[24:32].astype(F32), jnp.zeros((8, HD), F32)], axis=0).astype(BF16)
                out = out + jnp.dot(new, values, preferred_element_type=F32)
                out = out / weight_sum
                lse = jnp.broadcast_to(best + jnp.log(weight_sum), (16, HD))
                for t in range(2):
                    suf_out[pl.ds(4 * head + t, 8, stride=8)] = out[8 * t : 8 * t + 8]
                    suf_out[pl.ds(4 * head + 2 + t, 8, stride=8)] = lse[8 * t : 8 * t + 8]

            mine = pl.ds(pl.multiple_of(8 * y, 8), 8)

            @pl.loop(0, 15)
            def _(i):
                to_y, to_grp = y_peer(i // 2), lax.rem(i, 2)
                to = {"ctx": column(to_y), "grp": to_grp}
                send(suf_out.at[pl.ds(pl.multiple_of(8 * to_y, 8), 8)], suf_in.at[mine], 15, to)

            suf_in[mine] = suf_out[mine]

        @pl.when(first)
        def _():
            wait_bytes(lse_in.at[pl.ds(0, 7)], recv_sem.at[14])
            wait_bytes(suf_in, recv_sem.at[15])
            wait_bytes(o_in.at[pl.ds(0, 7)], recv_sem.at[13])

        @pl.when(late)
        def _():
            wait_bytes(lse_in, recv_sem.at[14])
            wait_bytes(suf_in.at[pl.ds(0, 56)], recv_sem.at[15])
            wait_bytes(o_in, recv_sem.at[13])

        lane = lax.broadcasted_iota(jnp.int32, (16, HD), 1)
        row = lax.broadcasted_iota(jnp.int32, (16, HD), 0)
        mine = lane == row + 16 * y
        own = y * NX + x
        for head in range(2):
            lses = [jnp.sum(jnp.where(mine, lse_in[i, head], 0.0), axis=1, keepdims=True) for i in range(8)]
            lses.append(jnp.concatenate([suf_in[pl.ds(4 * head + 2 + t, 8, stride=8)] for t in range(2)], axis=0)[:, 0:1])
            best = functools.reduce(jnp.maximum, lses)
            shares = [jnp.exp(v - best) for v in lses]
            outs = [o_in[i, head].astype(F32) for i in range(8)]
            outs.append(jnp.concatenate([suf_in[pl.ds(4 * head + t, 8, stride=8)] for t in range(2)], axis=0))
            att[own, head] = (total([o * s for o, s in zip(outs, shares)]) / total(shares)).astype(BF16)

        @pl.loop(0, 31)
        def _(i):
            to_x, to_y = plane_peer(i)
            send(att.at[own], att.at[own], 16, {"ctx": to_x * NY + to_y})

        loads[5].wait()
        wait_bytes(wo_v.at[0], recv_sem.at[5])

        @pl.when(late)
        def _():
            pl.semaphore_wait(last, 1)

        wait_bytes(att.at[pl.ds(0, 31)], recv_sem.at[16])
        projected = total(
            [
                jnp.dot(
                    jnp.concatenate([att[4 * j : 4 * j + 4, head].reshape(64, HD) for head in range(2)], axis=1),
                    jnp.concatenate([wo_v[head, HD * j : HD * j + HD] for head in range(2)], axis=0),
                    preferred_element_type=F32,
                )
                for j in range(8)
            ]
        )
        ordered = [projected[16 * b + 8 * t : 16 * b + 8 * t + 8] for t in range(2) for b in range(NX)]
        res[z] = jnp.concatenate(ordered, axis=0).astype(BF16)

        @pl.loop(0, 3)
        def _(i):
            send(res.at[z], res.at[z], 17, {"kvh": z_peer(i)})
            send(res.at[z], res.at[z], 17, {"kvh": z_peer(i) + 1})

        send(res.at[z], res.at[z], 17, {"kvh": lead - 1})

    wait_bytes(part_in.at[0, pl.ds(0, 3)], send_sem.at[0])

    @pl.when(first)
    def _():
        wait_bytes(kv_v.at[0, pl.ds(0, 3)], send_sem.at[4])

    @pl.when(late)
    def _():
        wait_bytes(direct_in.at[0], send_sem.at[6])

    @pl.when(helper)
    def _():
        wait_bytes(part_in.at[0, 3], send_sem.at[1])
        wait_bytes(head_bias.at[0], send_sem.at[2])
        wait_bytes(kv_v.at[0, 3], send_sem.at[3])
        wait_bytes(wo_v.at[0], send_sem.at[5])

    @pl.when(worker)
    def _():
        wait_bytes(sq_in, send_sem.at[8])

        @pl.when(first)
        def _():
            wait_bytes(mid_in, send_sem.at[9])
            wait_bytes(sq2_in, send_sem.at[10])
            wait_bytes(pairs_in.at[pl.ds(0, 8)], send_sem.at[11])
            wait_bytes(query.at[pl.ds(0, 7)], send_sem.at[12])
            wait_bytes(o_in, send_sem.at[13])
            wait_bytes(o_in.at[pl.ds(0, 7)], send_sem.at[13])
            wait_bytes(lse_in, send_sem.at[14])
            wait_bytes(lse_in.at[pl.ds(0, 7)], send_sem.at[14])

        @pl.when(late)
        def _():
            wait_bytes(direct_sq_in, send_sem.at[7])
            wait_bytes(sq2_in.at[pl.ds(0, 7)], send_sem.at[10])
            wait_bytes(pairs_in.at[pl.ds(0, 7)], send_sem.at[11])
            wait_bytes(suf_in, send_sem.at[15])
            wait_bytes(suf_in.at[pl.ds(0, 56)], send_sem.at[15])

        wait_bytes(att.at[pl.ds(0, 31)], send_sem.at[16])
        wait_bytes(res, send_sem.at[17])
        wait_bytes(res.at[pl.ds(0, 3)], send_sem.at[17])
        wait_bytes(res.at[pl.ds(0, 3)], recv_sem.at[17])

    @pl.when(helper)
    def _():
        wait_bytes(res, recv_sem.at[17])

    out_ref[...] = total([res[k].astype(F32) for k in range(4)]).astype(BF16).reshape(2, 32, HD)


def local(hidden_in, norm_gain, w_qkv, qkv_bias, kv_pool, suffix_lengths, w_out):
    anywhere = pl.BlockSpec(memory_space=pl.ANY)
    vmem = pltpu.VMEM
    return pl.pallas_call(
        kernel,
        out_shape=jax.ShapeDtypeStruct((2, 32, HD), BF16),
        in_specs=[anywhere] * 5 + [pl.BlockSpec(memory_space=pltpu.SMEM), anywhere],
        out_specs=pl.BlockSpec(memory_space=vmem),
        scratch_shapes=[
            vmem((2, 32, HD), BF16), vmem((HD,), BF16), vmem((HD, 1280), BF16), vmem((1, 1280), BF16),
            vmem((2, 4, 2, 512, HD), BF16), vmem((2, 1024, HD), BF16), vmem((2, 32, HD), F32), vmem((2, 256, HD), F32),
            vmem((4, 10, 16, HD), BF16), vmem((2, 4, 10, 16, HD), BF16), vmem((1, HD), F32), vmem((3, 1, HD), F32),
            vmem((2, 32, 16, HD), BF16), vmem((32, 1, HD), F32),
            vmem((8, 2, 16, HD), BF16), vmem((7, 2, 16, HD), BF16),
            vmem((8, 2, 32, HD), BF16), vmem((15, 2, 32, HD), BF16), vmem((1, HD), F32), vmem((15, 1, HD), F32),
            vmem((8, 2, 16, HD), BF16), vmem((8, 2, 16, HD), BF16), vmem((8, 2, 16, HD), BF16),
            vmem((2, 1, HD), F32), vmem((8, 2, 1, HD), F32), vmem((64, HD), F32), vmem((64, HD), F32),
            vmem((32, 2, 16, HD), BF16), vmem((4, 64, HD), BF16),
            pltpu.SemaphoreType.DMA((6,)), pltpu.SemaphoreType.DMA((18,)), pltpu.SemaphoreType.DMA((18,)),
            pltpu.SemaphoreType.REGULAR((5,)),
        ],
        compiler_params=pltpu.CompilerParams(
            collective_id=0, has_side_effects=True, vmem_limit_bytes=60 << 20
        ),
        name="attention_block",
    )(
        hidden_in, norm_gain, w_qkv.reshape(HD, 1280), qkv_bias, kv_pool.reshape(2, 512, HD),
        suffix_lengths, w_out,
    )


def solution(mesh):
    placed = (
        P(None, None, ("ctx", "grp")),
        P(("ctx", "grp")),
        P(("ctx", "grp"), "kvh", None),
        P("kvh", None),
        P("grp", None, "kvh", "ctx", None),
        P("ctx"),
        P("kvh", ("ctx", "grp")),
    )
    return jax.shard_map(
        local, mesh=mesh, in_specs=placed, out_specs=P(None, None, ("ctx", "grp")), check_vma=False
    )
```

time: 60.7 us -> 49.6 us (0.82)
  Pallas kernels: 58.6 us -> 47.3 us
    pallas_call x1, Pallas kernels: 58.6 us -> 47.3 us  [local(): pl.pallas_call(kernel, out_shape=jax.ShapeDtypeStruct((2, 32, HD), BF16),...]
where the time goes in v3:
time: 49.6 us; the launch traced here: 49.3 us
  Pallas kernels  47.3 us (95%)
  local copies, waits for them, and re-layouts  1.32 us (3%)
  between operations  0.66 us (1%)
    pallas_call x1, Pallas kernels, local(): pl.pallas_call(kernel, out_shape=jax.ShapeDtypeStruct((2, 32, HD), BF16),...  47.3 us
    unnamed x1, local copies, waits for them, and re-layouts  1.32 us

profile of v3, /device:TPU:1, one launch (start us, length us, event | category | flops | bytes accessed | tf_op | source)
XLA Modules:
  0.0 49.3 jit_solution(17327867205980556951)
XLA Ops:
  0.7 47.3 %attention_block.1 = bf16[2,32,128]{2,1,0:T(8,128)(2,1)} custom-call(bf16[2,32,128]{2,1,0:T(8,128)(2,1)} %h_any.1, bf16[128]{0:T(256)(128)(2,1)} %gain_any.1, bf16[128,1280]{1,0:T(8,128)(2,1)} %bitcast.2, bf16[1,1280]{1,0:T(2,128)(2,1)} %bias_any.1, bf16[2,512,128]{2,1,0:T(8,128)(2,1)} %bitcast.3, s32[1]{0:T(128)S(6)} %copy.9.len_ref, bf16[1024,128]{1,0:T(8,128)(2,1)} %wo_any.1), custom_call_target="tpu_custom_call" | custom-call | tf_op jit(solution)/shard_map/attention_block/pallas_call | solution.py:488
  48.0 1.3 %copy.10 = bf16[2,32,128]{2,1,0:T(8,128)(2,1)} copy(bf16[2,32,128]{2,1,0:T(8,128)(2,1)} %attention_block.1) | data formatting | bytes 32768

commit v4 on v3

--- a/solution.py
+++ b/solution.py
@@ -17,6 +17,8 @@
 
 
 def zigzag(k, middle):
+    if isinstance(k, int):
+        return middle + (1 - 2 * (k % 2)) * ((k + 1) // 2)
     return middle + (1 - 2 * lax.rem(k, 2)) * ((k + 1) // 2)
 
 
@@ -29,8 +31,8 @@
 
 
 def kernel(
-    h_any, gain_any, w_any, bias_any, kv_any, len_ref, wo_any, out_ref,
-    h_v, gain_v, w_v, bias_v, kv_v, wo_v, head_bias, rows,
+    h_any, gain_any, w_any, bias_any, kv_any, len_any, wo_any, out_ref,
+    h_v, gain_v, w_v, bias_v, kv_v, wo_v, len_ref, head_bias, rows,
     part, part_in, sq, sq_in, direct_in, direct_sq_in,
     mid, mid_in, pairs, pairs_in, sq2, sq2_in,
     query, o_out, o_in, lse_out, lse_in, suf_out, suf_in, att, res,
@@ -53,7 +55,7 @@
     loads = [
         pltpu.make_async_copy(src, dst, local_sem.at[i])
         for i, (src, dst) in enumerate(
-            ((h_any, h_v), (gain_any, gain_v), (w_any, w_v), (bias_any, bias_v), (kv_any, kv_v.at[1, 3]), (wo_any, wo_v.at[1]))
+            ((h_any, h_v), (gain_any, gain_v), (w_any, w_v), (bias_any, bias_v), (kv_any, kv_v.at[1, 3]), (wo_any, wo_v.at[1]), (len_any, len_ref))
         )
     ]
     for load in loads[:4]:
@@ -83,21 +85,21 @@
 
     @pl.when(worker)
     def _():
-        @pl.loop(0, 3)
+        @pl.loop(0, 3, unroll=True)
         def _(i):
             tell(barrier, {"ctx": x_peer(i)})
 
-        @pl.loop(0, 4)
+        @pl.loop(0, 4, unroll=True)
         def _(i):
             tell(barrier, {"ctx": x_peer(i), "kvh": lead - 1})
 
     @pl.when(worker & first)
     def _():
-        @pl.loop(0, 7)
+        @pl.loop(0, 7, unroll=True)
         def _(i):
             tell(barrier, {"ctx": column(y_peer(i))})
 
-        @pl.loop(0, 3)
+        @pl.loop(0, 3, unroll=True)
         def _(i):
             tell(barrier, {"kvh": z_peer(i) + 1})
 
@@ -105,12 +107,13 @@
     def _():
         loads[4].start()
         loads[5].start()
+        loads[6].start()
 
     @pl.when(worker & first)
     def _():
         pl.semaphore_wait(barrier, 13)
 
-        @pl.loop(0, 7)
+        @pl.loop(0, 7, unroll=True)
         def _(i):
             tell(plane, {"ctx": column(y_peer(i))})
 
@@ -142,7 +145,7 @@
     def _():
         pl.semaphore_wait(barrier, 4)
 
-        @pl.loop(0, 8)
+        @pl.loop(0, 8, unroll=True)
         def _(i):
             tell(hello, {"ctx": column(y_peer(i)), "grp": 0})
 
@@ -151,7 +154,7 @@
         pl.semaphore_wait(barrier, 5)
         tell(hello, {"kvh": lead, "grp": 0})
 
-    @pl.loop(0, 3)
+    @pl.loop(0, 3, unroll=True)
     def _(i):
         to = x_peer(i)
         send(part.at[to // NY], part_in.at[core, i], 0, {"ctx": to, "kvh": lead})
@@ -162,20 +165,20 @@
 
     @pl.when(worker)
     def _():
-        @pl.loop(0, 3)
+        @pl.loop(0, 3, unroll=True)
         def _(i):
             send(sq, sq_in.at[i], 8, {"ctx": x_peer(i)})
 
     @pl.when(late)
     def _():
-        @pl.loop(0, 32)
+        @pl.loop(0, 32, unroll=True)
         def _(i):
             to_x, to_y = plane_peer(i)
             send(part.at[to_x, to_y], direct_in.at[core, ctx], 6, {"ctx": to_x * NY + to_y, "kvh": lead, "grp": 0})
 
     @pl.when(late & worker)
     def _():
-        @pl.loop(0, 32)
+        @pl.loop(0, 32, unroll=True)
         def _(i):
             to_x, to_y = plane_peer(i)
             send(sq, direct_sq_in.at[ctx], 7, {"ctx": to_x * NY + to_y, "grp": 0})
@@ -198,7 +201,7 @@
 
     @pl.when(first)
     def _():
-        @pl.loop(0, 3)
+        @pl.loop(0, 3, unroll=True)
         def _(i):
             send(kv_any, kv_v.at[core, i], 4, {"ctx": x_peer(i), "kvh": lead})
 
@@ -229,7 +232,7 @@
             for head, line in enumerate(lines):
                 mid[:, head] = line[0:8].astype(BF16)
 
-            @pl.loop(0, 7)
+            @pl.loop(0, 7, unroll=True)
             def _(i):
                 to_y = y_peer(i)
                 send(mid.at[to_y], mid_in.at[i], 9, {"ctx": column(to_y)})
@@ -247,14 +250,14 @@
             pl.semaphore_wait(hello, 9)
             tell(go, {"grp": 1})
 
-            @pl.loop(0, 8)
+            @pl.loop(0, 8, unroll=True)
             def _(i):
                 to_y = y_peer(i)
                 to = {"ctx": column(to_y), "grp": 1}
                 send(pairs.at[to_y], pairs_in.at[7 + i], 11, to)
                 send(sq2, sq2_in.at[7 + i], 10, to)
 
-            @pl.loop(0, 3)
+            @pl.loop(0, 3, unroll=True)
             def _(i):
                 tell(ready, {"kvh": z_peer(i) + 1})
 
@@ -276,7 +279,7 @@
                 summed = total([direct_in[head, i].astype(F32) for i in range(32)]) + sums[head]
                 query[y, head] = (summed * inverse + head_bias[head, pl.ds(y, 1)]).astype(BF16)
 
-            @pl.loop(0, 7)
+            @pl.loop(0, 7, unroll=True)
             def _(i):
                 send(query.at[y], query.at[y], 12, {"ctx": column(y_peer(i))})
 
@@ -284,13 +287,14 @@
         def _():
             pl.semaphore_wait(go, 1)
 
-            @pl.loop(0, 7)
+            @pl.loop(0, 7, unroll=True)
             def _(i):
                 to_y = y_peer(i)
                 send(pairs.at[to_y], pairs_in.at[i], 11, {"ctx": column(to_y)})
                 send(sq2, sq2_in.at[i], 10, {"ctx": column(to_y)})
 
         loads[4].wait()
+        loads[6].wait()
 
         def scores_of(q, keys):
             return lax.dot_general(q, keys, (((1,), (1,)), ((), ())), preferred_element_type=F32) * factor
@@ -313,7 +317,7 @@
                 lse = best + jnp.log(weight_sum)
                 lse_out[head] = jnp.sum(jnp.where(lane == row, lse, 0.0), axis=0, keepdims=True)
 
-            @pl.loop(0, 15)
+            @pl.loop(0, 15, unroll=True)
             def _(i):
                 to_y, to_grp = y_peer(i // 2), 1 - lax.rem(i, 2)
                 to = {"ctx": column(to_y), "grp": to_grp}
@@ -364,7 +368,7 @@
 
             mine = pl.ds(pl.multiple_of(8 * y, 8), 8)
 
-            @pl.loop(0, 15)
+            @pl.loop(0, 15, unroll=True)
             def _(i):
                 to_y, to_grp = y_peer(i // 2), lax.rem(i, 2)
                 to = {"ctx": column(to_y), "grp": to_grp}
@@ -397,7 +401,7 @@
             outs.append(jnp.concatenate([suf_in[pl.ds(4 * head + t, 8, stride=8)] for t in range(2)], axis=0))
             att[own, head] = (total([o * s for o, s in zip(outs, shares)]) / total(shares)).astype(BF16)
 
-        @pl.loop(0, 31)
+        @pl.loop(0, 31, unroll=True)
         def _(i):
             to_x, to_y = plane_peer(i)
             send(att.at[own], att.at[own], 16, {"ctx": to_x * NY + to_y})
@@ -423,7 +427,7 @@
         ordered = [projected[16 * b + 8 * t : 16 * b + 8 * t + 8] for t in range(2) for b in range(NX)]
         res[z] = jnp.concatenate(ordered, axis=0).astype(BF16)
 
-        @pl.loop(0, 3)
+        @pl.loop(0, 3, unroll=True)
         def _(i):
             send(res.at[z], res.at[z], 17, {"kvh": z_peer(i)})
             send(res.at[z], res.at[z], 17, {"kvh": z_peer(i) + 1})
@@ -488,11 +492,11 @@
     return pl.pallas_call(
         kernel,
         out_shape=jax.ShapeDtypeStruct((2, 32, HD), BF16),
-        in_specs=[anywhere] * 5 + [pl.BlockSpec(memory_space=pltpu.SMEM), anywhere],
+        in_specs=[anywhere] * 7,
         out_specs=pl.BlockSpec(memory_space=vmem),
         scratch_shapes=[
             vmem((2, 32, HD), BF16), vmem((HD,), BF16), vmem((HD, 1280), BF16), vmem((1, 1280), BF16),
-            vmem((2, 4, 2, 512, HD), BF16), vmem((2, 1024, HD), BF16), vmem((2, 32, HD), F32), vmem((2, 256, HD), F32),
+            vmem((2, 4, 2, 512, HD), BF16), vmem((2, 1024, HD), BF16), pltpu.SMEM((1,), jnp.int32), vmem((2, 32, HD), F32), vmem((2, 256, HD), F32),
             vmem((4, 10, 16, HD), BF16), vmem((2, 4, 10, 16, HD), BF16), vmem((1, HD), F32), vmem((3, 1, HD), F32),
             vmem((2, 32, 16, HD), BF16), vmem((32, 1, HD), F32),
             vmem((8, 2, 16, HD), BF16), vmem((7, 2, 16, HD), BF16),
@@ -500,7 +504,7 @@
             vmem((8, 2, 16, HD), BF16), vmem((8, 2, 16, HD), BF16), vmem((8, 2, 16, HD), BF16),
             vmem((2, 1, HD), F32), vmem((8, 2, 1, HD), F32), vmem((64, HD), F32), vmem((64, HD), F32),
             vmem((32, 2, 16, HD), BF16), vmem((4, 64, HD), BF16),
-            pltpu.SemaphoreType.DMA((6,)), pltpu.SemaphoreType.DMA((18,)), pltpu.SemaphoreType.DMA((18,)),
+            pltpu.SemaphoreType.DMA((7,)), pltpu.SemaphoreType.DMA((18,)), pltpu.SemaphoreType.DMA((18,)),
             pltpu.SemaphoreType.REGULAR((5,)),
         ],
         compiler_params=pltpu.CompilerParams(

time: 49.6 us -> 49 us (0.988)
  Pallas kernels: 47.3 us -> 46.7 us
    pallas_call x1, Pallas kernels: 47.3 us -> 46.7 us  [local(): pl.pallas_call(kernel, out_shape=jax.ShapeDtypeStruct((2, 32, HD), BF16),...]
where the time goes in v4:
time: 49 us; the launch traced here: 48.7 us
  Pallas kernels  46.7 us (95%)
  local copies, waits for them, and re-layouts  1.32 us (3%)
  between operations  0.66 us (1%)
    pallas_call x1, Pallas kernels, local(): pl.pallas_call(kernel, out_shape=jax.ShapeDtypeStruct((2, 32, HD), BF16),...  46.7 us
    unnamed x1, local copies, waits for them, and re-layouts  1.32 us

profile of v4, /device:TPU:1, one launch (start us, length us, event | category | flops | bytes accessed | tf_op | source)
XLA Modules:
  0.0 48.7 jit_solution(4227735121632893807)
XLA Ops:
  0.7 46.7 %attention_block.1 = bf16[2,32,128]{2,1,0:T(8,128)(2,1)} custom-call(bf16[2,32,128]{2,1,0:T(8,128)(2,1)} %h_any.1, bf16[128]{0:T(256)(128)(2,1)} %gain_any.1, bf16[128,1280]{1,0:T(8,128)(2,1)} %bitcast.2, bf16[1,1280]{1,0:T(2,128)(2,1)} %bias_any.1, bf16[2,512,128]{2,1,0:T(8,128)(2,1)} %bitcast.3, s32[1]{0:T(128)S(6)} %copy.9.len_any, bf16[1024,128]{1,0:T(8,128)(2,1)} %wo_any.1), custom_call_target="tpu_custom_call" | custom-call | tf_op jit(solution)/shard_map/attention_block/pallas_call | solution.py:492
  47.4 1.3 %copy.10 = bf16[2,32,128]{2,1,0:T(8,128)(2,1)} copy(bf16[2,32,128]{2,1,0:T(8,128)(2,1)} %attention_block.1) | data formatting | bytes 32768

commit v5 on v4

--- a/solution.py
+++ b/solution.py
@@ -169,19 +169,12 @@
         def _(i):
             send(sq, sq_in.at[i], 8, {"ctx": x_peer(i)})
 
-    @pl.when(late)
+    @pl.when(late & helper)
     def _():
         @pl.loop(0, 32, unroll=True)
         def _(i):
             to_x, to_y = plane_peer(i)
             send(part.at[to_x, to_y], direct_in.at[core, ctx], 6, {"ctx": to_x * NY + to_y, "kvh": lead, "grp": 0})
-
-    @pl.when(late & worker)
-    def _():
-        @pl.loop(0, 32, unroll=True)
-        def _(i):
-            to_x, to_y = plane_peer(i)
-            send(sq, direct_sq_in.at[ctx], 7, {"ctx": to_x * NY + to_y, "grp": 0})
 
     loads[3].wait()
     for j in range(8):
@@ -217,6 +210,16 @@
 
     @pl.when(worker)
     def _():
+
+        @pl.when(late)
+        def _():
+            @pl.loop(0, 32, unroll=True)
+            def _(i):
+                to_x, to_y = plane_peer(i)
+                to = {"ctx": to_x * NY + to_y, "grp": 0}
+                send(sq, direct_sq_in.at[ctx], 7, to)
+                send(part.at[to_x, to_y], direct_in.at[core, ctx], 6, to)
+
         rows[...] = jnp.zeros_like(rows)
         wait_bytes(sq_in, recv_sem.at[8])
         sq2[...] = total([sq_in[i] for i in range(3)]) + sq[...]

time: 49 us -> 48.9 us (level)
  no operation moved by 1% of the time
where the time goes in v5:
time: 48.9 us; the launch traced here: 48.6 us
  Pallas kernels  46.6 us (95%)
  local copies, waits for them, and re-layouts  1.32 us (3%)
  between operations  0.66 us (1%)
    pallas_call x1, Pallas kernels, local(): pl.pallas_call(kernel, out_shape=jax.ShapeDtypeStruct((2, 32, HD), BF16),...  46.6 us
    unnamed x1, local copies, waits for them, and re-layouts  1.32 us

profile of v5, /device:TPU:1, one launch (start us, length us, event | category | flops | bytes accessed | tf_op | source)
XLA Modules:
  0.0 48.6 jit_solution(13718905465540614548)
XLA Ops:
  0.7 46.6 %attention_block.1 = bf16[2,32,128]{2,1,0:T(8,128)(2,1)} custom-call(bf16[2,32,128]{2,1,0:T(8,128)(2,1)} %h_any.1, bf16[128]{0:T(256)(128)(2,1)} %gain_any.1, bf16[128,1280]{1,0:T(8,128)(2,1)} %bitcast.2, bf16[1,1280]{1,0:T(2,128)(2,1)} %bias_any.1, bf16[2,512,128]{2,1,0:T(8,128)(2,1)} %bitcast.3, s32[1]{0:T(128)S(6)} %copy.9.len_any, bf16[1024,128]{1,0:T(8,128)(2,1)} %wo_any.1), custom_call_target="tpu_custom_call" | custom-call | tf_op jit(solution)/shard_map/attention_block/pallas_call | solution.py:495
  47.3 1.3 %copy.10 = bf16[2,32,128]{2,1,0:T(8,128)(2,1)} copy(bf16[2,32,128]{2,1,0:T(8,128)(2,1)} %attention_block.1) | data formatting | bytes 32768

commit v6 on v4

--- a/solution.py
+++ b/solution.py
@@ -157,7 +157,8 @@
     @pl.loop(0, 3, unroll=True)
     def _(i):
         to = x_peer(i)
-        send(part.at[to // NY], part_in.at[core, i], 0, {"ctx": to, "kvh": lead})
+        for c in range(0, 10, 2):
+            send(part.at[to // NY, pl.ds(c, 2)], part_in.at[core, i, pl.ds(c, 2)], 0, {"ctx": to, "kvh": lead})
 
     @pl.when(helper)
     def _():

time: 49 us -> 49 us (level)
  no operation moved by 1% of the time
where the time goes in v6:
time: 49 us; the launch traced here: 48.7 us
  Pallas kernels  46.7 us (95%)
  local copies, waits for them, and re-layouts  1.32 us (3%)
  between operations  0.66 us (1%)
    pallas_call x1, Pallas kernels, local(): pl.pallas_call(kernel, out_shape=jax.ShapeDtypeStruct((2, 32, HD), BF16),...  46.7 us
    unnamed x1, local copies, waits for them, and re-layouts  1.32 us

profile of v6, /device:TPU:1, one launch (start us, length us, event | category | flops | bytes accessed | tf_op | source)
XLA Modules:
  0.0 48.7 jit_solution(6530854812827135607)
XLA Ops:
  0.7 46.7 %attention_block.1 = bf16[2,32,128]{2,1,0:T(8,128)(2,1)} custom-call(bf16[2,32,128]{2,1,0:T(8,128)(2,1)} %h_any.1, bf16[128]{0:T(256)(128)(2,1)} %gain_any.1, bf16[128,1280]{1,0:T(8,128)(2,1)} %bitcast.2, bf16[1,1280]{1,0:T(2,128)(2,1)} %bias_any.1, bf16[2,512,128]{2,1,0:T(8,128)(2,1)} %bitcast.3, s32[1]{0:T(128)S(6)} %copy.9.len_any, bf16[1024,128]{1,0:T(8,128)(2,1)} %wo_any.1), custom_call_target="tpu_custom_call" | custom-call | tf_op jit(solution)/shard_map/attention_block/pallas_call | solution.py:493
  47.4 1.3 %copy.10 = bf16[2,32,128]{2,1,0:T(8,128)(2,1)} copy(bf16[2,32,128]{2,1,0:T(8,128)(2,1)} %attention_block.1) | data formatting | bytes 32768
